TPU v7x, 128 devices: a whole 4x4x4 slice. The times are simulated.
128 devices in a mesh: seq: 16 (over x, y_lo, core), fsdp: 8 (over y_hi, z).
Axes of the slice: x: 4, y: 4 (y_hi: 2, y_lo: 2; y = y_hi * 2 + y_lo), z: 4, core: 2. Of those that a mesh axis runs over, the one named last changes fastest.
Arguments:
- block_in: float32 [8, 8192, 640], P('fsdp', 'seq'), may hold values from -6 to 6
- seg_ids: int32 [8, 8192], P('fsdp', 'seq'), may hold values from 0 to 2, as said below
- cotangent: float32 [8, 8192, 640], P('fsdp', 'seq'), may hold values from -6 to 6
- query_weight: float32 [640, 1024], P(('seq', 'fsdp')), may hold values from -0.25 to 0.25
- query_mean: float32 [640, 1024], P(('seq', 'fsdp')), may hold values from -160 to 160
- query_square: float32 [640, 1024], P(('seq', 'fsdp')), may hold values from 3276.8 to 26214.4
- keyval_weight: float32 [640, 512], P(('seq', 'fsdp')), may hold values from -0.25 to 0.25
- keyval_mean: float32 [640, 512], P(('seq', 'fsdp')), may hold values from -512 to 512
- keyval_square: float32 [640, 512], P(('seq', 'fsdp')), may hold values from 29491.2 to 235929.6
- output_weight: float32 [1024, 640], P(('seq', 'fsdp')), may hold values from -4 to 4
- output_mean: float32 [1024, 640], P(('seq', 'fsdp')), may hold values from -8 to 8
- output_square: float32 [1024, 640], P(('seq', 'fsdp')), may hold values from 8.192 to 65.536
- gateup_weight: float32 [640, 4096], P(('seq', 'fsdp')), may hold values from -0.25 to 0.25
- gateup_mean: float32 [640, 4096], P(('seq', 'fsdp')), may hold values from -56 to 56
- gateup_square: float32 [640, 4096], P(('seq', 'fsdp')), may hold values from 373.5552 to 3080.192
- down_weight: float32 [2048, 640], P(('seq', 'fsdp')), may hold values from -0.125 to 0.125
- down_mean: float32 [2048, 640], P(('seq', 'fsdp')), may hold values from -96 to 96
- down_square: float32 [2048, 640], P(('seq', 'fsdp')), may hold values from 1179.648 to 9437.184
- norm_gains: float32 [2, 640], P(None, ('seq', 'fsdp')), may hold values from 0.5 to 1.5
- gains_mean: float32 [2, 640], P(None, ('seq', 'fsdp')), may hold values from -320 to 320
- gains_square: float32 [2, 640], P(None, ('seq', 'fsdp')), may hold values from 13107.2 to 104857.6
Outputs:
- block_out: float32 [8, 8192, 640], P('fsdp', 'seq')
- input_grad: float32 [8, 8192, 640], P('fsdp', 'seq')
- query_mean_new: float32 [640, 1024], P(('seq', 'fsdp'))
- query_square_new: float32 [640, 1024], P(('seq', 'fsdp'))
- query_weight_new: float32 [640, 1024], P(('seq', 'fsdp'))
- keyval_mean_new: float32 [640, 512], P(('seq', 'fsdp'))
- keyval_square_new: float32 [640, 512], P(('seq', 'fsdp'))
- keyval_weight_new: float32 [640, 512], P(('seq', 'fsdp'))
- output_mean_new: float32 [1024, 640], P(('seq', 'fsdp'))
- output_square_new: float32 [1024, 640], P(('seq', 'fsdp'))
- output_weight_new: float32 [1024, 640], P(('seq', 'fsdp'))
- gateup_mean_new: float32 [640, 4096], P(('seq', 'fsdp'))
- gateup_square_new: float32 [640, 4096], P(('seq', 'fsdp'))
- gateup_weight_new: float32 [640, 4096], P(('seq', 'fsdp'))
- down_mean_new: float32 [2048, 640], P(('seq', 'fsdp'))
- down_square_new: float32 [2048, 640], P(('seq', 'fsdp'))
- down_weight_new: float32 [2048, 640], P(('seq', 'fsdp'))
- gains_mean_new: float32 [2, 640], P(None, ('seq', 'fsdp'))
- gains_square_new: float32 [2, 640], P(None, ('seq', 'fsdp'))
- norm_gains_new: float32 [2, 640], P(None, ('seq', 'fsdp'))
Inputs may be any that keep to these rules, and one draw needn't show every extreme that they name: `seg_ids`: document numbers never fall along a sequence, and every sequence holds documents 0, 1 and 2.
All inputs are finite; a program needn't handle non-finite values.
Results may differ from a plain program's by a relative error of at most 0.015.
Values may be sent and summed in bfloat16 or wider, within the bound.
No kernel may reach another device: no remote copies, remote signals or barrier semaphores. Data moves between devices by JAX's collectives and lax.ppermute only.
A program may use at most 128 MiB of HBM per device.

v0:
```python
import jax
import jax.numpy as jnp
from jax import lax
from jax.sharding import PartitionSpec as P

D = 640
HQ = 4
HD = 256
FF = 2048
WINDOW = 512
STEP = 5


EPS_NORM = 1e-06
BETA_ONE = 0.9
BETA_TWO = 0.95
ADAM_EPS = 1e-08
DECAY = 0.1
GAIN_RATE = 0.5
RATE_FACTOR = 0.7
MASKED = -1e30


def passed_along(value, axis, by):
    peers = lax.axis_size(axis)
    pairs = [(i, i + by) for i in range(peers) if 0 <= i + by < peers]
    return lax.ppermute(value, axis, pairs)


def rms_scale(values, gain):
    return values * lax.rsqrt(jnp.mean(values * values, axis=-1, keepdims=True) + EPS_NORM) * gain


def product(form, left, right):
    return jnp.einsum(form, left, right, preferred_element_type=jnp.float32)


def adamw_step(weight, mean_old, square_old, gradient, rate, decay):
    mean_new = BETA_ONE * mean_old + (1.0 - BETA_ONE) * gradient
    square_new = BETA_TWO * square_old + (1.0 - BETA_TWO) * gradient * gradient
    mean_hat = mean_new / (1.0 - BETA_ONE**STEP)
    square_hat = square_new / (1.0 - BETA_TWO**STEP)
    weight_new = weight - rate * (mean_hat / (jnp.sqrt(square_hat) + ADAM_EPS) + decay * weight)
    return (mean_new, square_new, weight_new)


def gelu_tanh(inputs):
    return jax.nn.gelu(inputs, approximate=True)


def local(
    block_in,
    seg_ids,
    cotangent,
    query_weight,
    query_mean,
    query_square,
    keyval_weight,
    keyval_mean,
    keyval_square,
    output_weight,
    output_mean,
    output_square,
    gateup_weight,
    gateup_mean,
    gateup_square,
    down_weight,
    down_mean,
    down_square,
    norm_gains,
    gains_mean,
    gains_square,
):
    tokens_in = block_in[0]
    seg_row = seg_ids[0]
    count = tokens_in.shape[0]
    hops = (WINDOW + count - 2) // count
    key_count = (hops + 1) * count
    scale = HD ** (-0.5)
    fetched = (
        lax.all_gather(query_weight.astype(jnp.bfloat16), ("seq", "fsdp"), axis=0, tiled=True),
        lax.all_gather(keyval_weight.astype(jnp.bfloat16), ("seq", "fsdp"), axis=0, tiled=True),
        lax.all_gather(output_weight.astype(jnp.bfloat16), ("seq", "fsdp"), axis=0, tiled=True),
        lax.all_gather(gateup_weight.astype(jnp.bfloat16), ("seq", "fsdp"), axis=0, tiled=True),
        lax.all_gather(down_weight.astype(jnp.bfloat16), ("seq", "fsdp"), axis=0, tiled=True),
        lax.all_gather(norm_gains.astype(jnp.bfloat16), ("seq", "fsdp"), axis=1, tiled=True),
    )
    query_full, keyval_full, output_full, gateup_full, down_full, gains_full = fetched
    gain_one = gains_full[0].astype(jnp.float32)
    gain_two = gains_full[1].astype(jnp.float32)
    hidden_one = rms_scale(tokens_in, gain_one).astype(jnp.bfloat16)
    queries = jnp.dot(hidden_one, query_full, preferred_element_type=jnp.float32).astype(
        jnp.bfloat16
    )
    keyvals = jnp.dot(hidden_one, keyval_full, preferred_element_type=jnp.float32).astype(
        jnp.bfloat16
    )
    id_values = seg_row.astype(jnp.bfloat16)
    arrived = [passed_along((keyvals, id_values), "seq", 1)]
    keys_all = jnp.concatenate([piece[0] for piece in arrived] + [keyvals], axis=0)
    ids_all = jnp.concatenate([piece[1] for piece in arrived] + [id_values], axis=0)
    sources = lax.axis_index("seq") - (hops - jnp.arange(hops + 1, dtype=jnp.int32))
    source_ok = jnp.repeat(sources >= 0, count)
    spread = (
        jnp.arange(count, dtype=jnp.int32)[:, None]
        - jnp.arange(key_count, dtype=jnp.int32)[None, :]
        + hops * count
    )
    allowed = (
        (spread >= 0)
        & (spread < WINDOW)
        & (id_values[:, None] == ids_all[None, :])
        & source_ok[None, :]
    )
    key_part = keys_all[:, :HD]
    value_part = keys_all[:, HD:]
    query_heads = queries.reshape(count, HQ, HD)

    def masked_scores():
        raw = product("thd,jd->htj", query_heads, key_part) * scale
        return jnp.where(allowed[None], raw, MASKED)

    scores = masked_scores()
    peak = jnp.max(scores, axis=-1, keepdims=True)
    exponent = jnp.exp(scores - peak)
    total = jnp.sum(exponent, axis=-1, keepdims=True)
    log_total = peak + jnp.log(total)
    probs_low = (exponent / total).astype(jnp.bfloat16)
    attended = (
        product("htj,jd->thd", probs_low, value_part).reshape(count, HQ * HD).astype(jnp.bfloat16)
    )
    middle = tokens_in + jnp.dot(attended, output_full, preferred_element_type=jnp.float32)
    hidden_two = rms_scale(middle, gain_two).astype(jnp.bfloat16)
    gateup = jnp.dot(hidden_two, gateup_full, preferred_element_type=jnp.float32)
    gate_part = gateup[:, :FF]
    up_part = gateup[:, FF:]
    gelu_value, gelu_pull = jax.vjp(gelu_tanh, gate_part)
    inner = (gelu_value * up_part).astype(jnp.bfloat16)
    block_out = middle + jnp.dot(inner, down_full, preferred_element_type=jnp.float32)
    fetched_back = (
        lax.all_gather(query_weight.astype(jnp.bfloat16), ("seq", "fsdp"), axis=0, tiled=True),
        lax.all_gather(keyval_weight.astype(jnp.bfloat16), ("seq", "fsdp"), axis=0, tiled=True),
        lax.all_gather(output_weight.astype(jnp.bfloat16), ("seq", "fsdp"), axis=0, tiled=True),
        lax.all_gather(gateup_weight.astype(jnp.bfloat16), ("seq", "fsdp"), axis=0, tiled=True),
        lax.all_gather(down_weight.astype(jnp.bfloat16), ("seq", "fsdp"), axis=0, tiled=True),
        lax.all_gather(norm_gains.astype(jnp.bfloat16), ("seq", "fsdp"), axis=1, tiled=True),
    )
    query_again, keyval_again, output_again, gateup_again, down_again, gains_again = fetched_back
    upstream = cotangent[0]
    down_back = upstream.astype(jnp.bfloat16)
    down_sum = product("tf,td->fd", inner, down_back)
    inner_back = product("td,fd->tf", down_back, down_again)
    gate_back = gelu_pull(inner_back * up_part)[0]
    gateup_back = jnp.concatenate([gate_back, inner_back * gelu_value], axis=1).astype(jnp.bfloat16)
    gateup_sum = product("td,tf->df", hidden_two, gateup_back)
    two_back = product("tf,df->td", gateup_back, gateup_again)
    norm_two_value, norm_two_pull = jax.vjp(rms_scale, middle, gain_two)
    middle_norm_back, gain_two_sum = norm_two_pull(two_back)
    middle_back = upstream + middle_norm_back
    branch_back = middle_back.astype(jnp.bfloat16)
    output_sum = product("tk,td->kd", attended, branch_back)
    attended_back = (
        product("td,kd->tk", branch_back, output_again).astype(jnp.bfloat16).reshape(count, HQ, HD)
    )
    probs = jnp.exp(masked_scores() - log_total)
    prob_back = product("thd,jd->htj", attended_back, value_part)
    value_back = product("htj,thd->jd", probs.astype(jnp.bfloat16), attended_back)
    scores_back = (probs * (prob_back - jnp.sum(probs * prob_back, axis=-1, keepdims=True))).astype(
        jnp.bfloat16
    )
    queries_back = (
        (product("htj,jd->thd", scores_back, key_part) * scale)
        .reshape(count, HQ * HD)
        .astype(jnp.bfloat16)
    )
    key_back = product("htj,thd->jd", scores_back, query_heads) * scale
    keyval_back_all = jnp.concatenate([key_back, value_back], axis=1)
    own_back = keyval_back_all[hops * count :]
    own_back = own_back + passed_along(
        keyval_back_all[(hops - 1) * count : (hops - 1 + 1) * count].astype(jnp.bfloat16), "seq", -1
    ).astype(jnp.float32)
    keyvals_back = own_back.astype(jnp.bfloat16)
    query_sum = product("td,tc->dc", hidden_one, queries_back)
    keyval_sum = product("td,tc->dc", hidden_one, keyvals_back)
    one_back = product("tc,dc->td", queries_back, query_again) + product(
        "tc,dc->td", keyvals_back, keyval_again
    )
    norm_one_value, norm_one_pull = jax.vjp(rms_scale, tokens_in, gain_one)
    input_norm_back, gain_one_sum = norm_one_pull(one_back)
    input_grad = middle_back + input_norm_back
    gains_stack = jnp.stack([gain_one_sum, gain_two_sum])
    summed = (
        lax.psum_scatter(query_sum, ("seq", "fsdp"), scatter_dimension=0, tiled=True),
        lax.psum_scatter(keyval_sum, ("seq", "fsdp"), scatter_dimension=0, tiled=True),
        lax.psum_scatter(output_sum, ("seq", "fsdp"), scatter_dimension=0, tiled=True),
        lax.psum_scatter(gateup_sum, ("seq", "fsdp"), scatter_dimension=0, tiled=True),
        lax.psum_scatter(down_sum, ("seq", "fsdp"), scatter_dimension=0, tiled=True),
        lax.psum_scatter(gains_stack, ("seq", "fsdp"), scatter_dimension=1, tiled=True),
    )
    query_new = adamw_step(
        query_weight, query_mean, query_square, summed[0], RATE_FACTOR * D ** (-0.5), DECAY
    )
    keyval_new = adamw_step(
        keyval_weight, keyval_mean, keyval_square, summed[1], RATE_FACTOR * D ** (-0.5), DECAY
    )
    output_new = adamw_step(
        output_weight,
        output_mean,
        output_square,
        summed[2],
        RATE_FACTOR * (HQ * HD // WINDOW) ** (-0.5),
        DECAY,
    )
    gateup_new = adamw_step(
        gateup_weight, gateup_mean, gateup_square, summed[3], RATE_FACTOR * D ** (-0.5), DECAY
    )
    down_new = adamw_step(
        down_weight, down_mean, down_square, summed[4], RATE_FACTOR * FF ** (-0.5), DECAY
    )
    gains_new = adamw_step(norm_gains, gains_mean, gains_square, summed[5], GAIN_RATE, 0.0)
    return (
        block_out[None],
        input_grad[None],
        query_new[0],
        query_new[1],
        query_new[2],
        keyval_new[0],
        keyval_new[1],
        keyval_new[2],
        output_new[0],
        output_new[1],
        output_new[2],
        gateup_new[0],
        gateup_new[1],
        gateup_new[2],
        down_new[0],
        down_new[1],
        down_new[2],
        gains_new[0],
        gains_new[1],
        gains_new[2],
    )


def solution(mesh):
    return jax.shard_map(
        local,
        mesh=mesh,
        in_specs=(
            P("fsdp", "seq", None),
            P("fsdp", "seq"),
            P("fsdp", "seq", None),
            P(("seq", "fsdp"), None),
            P(("seq", "fsdp"), None),
            P(("seq", "fsdp"), None),
            P(("seq", "fsdp"), None),
            P(("seq", "fsdp"), None),
            P(("seq", "fsdp"), None),
            P(("seq", "fsdp"), None),
            P(("seq", "fsdp"), None),
            P(("seq", "fsdp"), None),
            P(("seq", "fsdp"), None),
            P(("seq", "fsdp"), None),
            P(("seq", "fsdp"), None),
            P(("seq", "fsdp"), None),
            P(("seq", "fsdp"), None),
            P(("seq", "fsdp"), None),
            P(None, ("seq", "fsdp")),
            P(None, ("seq", "fsdp")),
            P(None, ("seq", "fsdp")),
        ),
        out_specs=(
            P("fsdp", "seq", None),
            P("fsdp", "seq", None),
            P(("seq", "fsdp"), None),
            P(("seq", "fsdp"), None),
            P(("seq", "fsdp"), None),
            P(("seq", "fsdp"), None),
            P(("seq", "fsdp"), None),
            P(("seq", "fsdp"), None),
            P(("seq", "fsdp"), None),
            P(("seq", "fsdp"), None),
            P(("seq", "fsdp"), None),
            P(("seq", "fsdp"), None),
            P(("seq", "fsdp"), None),
            P(("seq", "fsdp"), None),
            P(("seq", "fsdp"), None),
            P(("seq", "fsdp"), None),
            P(("seq", "fsdp"), None),
            P(None, ("seq", "fsdp")),
            P(None, ("seq", "fsdp")),
            P(None, ("seq", "fsdp")),
        ),
        check_vma=False,
    )
```

profile of v0, /device:TPU:0, one launch (start us, length us, event | category | flops | bytes accessed | tf_op | source)
XLA Modules:
  0.0 2160.9 jit_solution(12122640153432567643)
XLA Ops:
  7.2 1.4 convert_bitcast_fusion.1
  8.7 1.3 convert_element_type.115
  10.1 1.5 convert_bitcast_fusion
  11.7 1.4 convert_element_type.119
  13.8 316.5 %all-gather = bf16[128,5,2]{1,2,0:T(2,128)(2,1)S(1)} all-gather(bf16[1,5,2]{1,2,0:T(2,128)(2,1)S(1)} %convert_bitcast_fusion.3), channel_id=1, replica_groups=mesh['seq'=16,'fsdp'=8] {'seq','fsdp'}, dimensions={0}, use_global_device_ids=true | all-gather | bytes 2580 | tf_op jit(solution)/shard_map/all_gather | solution.py:86
  330.6 1.6 fusion.32
  333.0 315.5 %all-gather.1 = bf16[128,5,512]{2,1,0:T(8,128)(2,1)S(1)} all-gather(bf16[1,5,512]{2,1,0:T(8,128)(2,1)S(1)} %convert_bitcast_fusion.2), channel_id=1, replica_groups=mesh['seq'=16,'fsdp'=8] {'seq','fsdp'}, dimensions={0}, use_global_device_ids=true | all-gather | bytes 660480 | tf_op jit(solution)/shard_map/all_gather | solution.py:82
  649.0 1.4 convolution_convert_fusion.2
  650.4 2.1 collective-permute-start
  652.5 1.5 collective-permute-start.1
  654.7 1.8 fusion.22
  656.5 2.6 reshape.199
  659.2 2.0 convolution_convert_fusion.1
  661.1 2.3 copy.83
  663.5 2.9 fusion.81
  667.6 2.1 copy-done
  669.7 3.6 fusion.23
  673.3 2.7 multiply_reduce_fusion.3
  676.0 249.9 %all-gather.15.cloned.1.call-done = bf16[128,5,4096]{2,1,0:T(8,128)(2,1)} async-done(((bf16[1,5,4096]{2,1,0:T(8,128)(2,1)}), bf16[128,5,4096]{2,1,0:T(8,128)(2,1)}) %all-gather.15.cloned.1.call-update) | async-done | bytes 5242896 | tf_op jit(solution)/shard_map/all_gather | solution.py:84
  925.9 8.8 reshape.201
  934.7 8.2 fusion.72
  942.9 289.1 %all-gather.11.cloned.1.call-done = bf16[2048,640]{1,0:T(8,128)(2,1)} async-done(((bf16[16,640]{1,0:T(8,128)(2,1)}), bf16[2048,640]{1,0:T(8,128)(2,1)}) %all-gather.11.cloned.1.call-update) | async-done | bytes 2621456 | tf_op jit(solution)/shard_map/all_gather | solution.py:85
  1232.0 9.5 fusion.11
  1241.5 3.6 multiply_reduce_fusion
  1246.5 2.0 convolution_convert_fusion
  1248.6 2.3 copy.84
  1250.9 5.1 fusion.24
  1256.0 5.4 fusion
  1261.5 2.4 fusion.2
  1265.3 1.3 collective-permute-start.2
  1266.6 2.3 multiply_convert_fusion.2
  1268.9 2.6 fusion.39
  1271.5 2.4 fusion.48
  1274.3 5.8 fusion.16
  1281.2 1.6 fusion.88
  1282.9 6.1 fusion.83
  1289.1 2.8 fusion.87
  1291.9 4.7 fusion.28
  1296.6 1.9 multiply_reduce_fusion.1
  1298.5 68.4 %all-reduce.4 = f32[2,640]{1,0:T(2,128)S(1)} all-reduce(f32[2,640]{1,0:T(2,128)S(1)} %pad_maximum_fusion.5), channel_id=7, replica_groups=mesh['seq'=16,'fsdp'=8] {'seq','fsdp'}, use_global_device_ids=true, to_apply=%region_14.15.clone | all-reduce | flops 1280 | bytes 10240
  1367.8 2.9 fusion.31
  1370.6 135.0 %all-reduce.8.cloned.1.call-done = (f32[640,1024]{1,0:T(8,128)}, f32[640,512]{1,0:T(8,128)}, f32[1024,640]{1,0:T(8,128)}, f32[640,4096]{1,0:T(8,128)}) async-done(((f32[640,1024]{1,0:T(8,128)}, f32[640,512]{1,0:T(8,128)}, f32[1024,640]{1,0:T(8,128)}, f32[640,4096]{1,0:T(8,128)}), (f32[640,1024]{1,0:T(8,128)}, f32[640,512]{1,0:T(8,128)}, f32[1024,640]{1,0:T(8,128)}, ...) | async-done | bytes 17039376
  1505.6 1.4 multiply_subtract_fusion.4
  1507.0 1.4 multiply_subtract_fusion.3
  1508.4 1.5 multiply_subtract_fusion.2
  1509.9 1.8 multiply_subtract_fusion
  1511.7 640.9 %reduce-scatter.3.cloned.1.call-done = f32[16,640]{1,0:T(8,128)} async-done(((f32[2048,640]{1,0:T(8,128)}), f32[16,640]{1,0:T(8,128)}) %reduce-scatter.3.cloned.1.call-update) | async-done | bytes 40976 | tf_op jit(solution)/shard_map/reduce_scatter | solution.py:197
  2152.6 1.4 multiply_subtract_fusion.1
  (131 shorter events, 9.4 us)
Async XLA Ops:
  7.2 649.3 %all-gather.13.cloned.1.call-start = ((), (), s32[]{:S(2)}) async-start(), calls=%async_computation.4 | async-start | bytes 2113536 | tf_op jit(solution)/shard_map/all_gather | solution.py:81
  8.6 664.6 %all-gather.9.cloned.1.call-start = ((), (), s32[]{:S(2)}) async-start(), calls=%async_computation.1 | async-start | bytes 1320960 | tf_op jit(solution)/shard_map/all_gather | solution.py:83
  10.0 915.9 %all-gather.15.cloned.1.call-start = ((), (), s32[]{:S(2)}) async-start(), calls=%async_computation.5 | async-start | bytes 8454144 | tf_op jit(solution)/shard_map/all_gather | solution.py:84
  11.7 1220.4 %all-gather.11.cloned.1.call-start = ((), (), s32[]{:S(2)}) async-start(), calls=%async_computation.2 | async-start | bytes 2641920 | tf_op jit(solution)/shard_map/all_gather | solution.py:85
  13.1 1492.5 %all-reduce.8.cloned.1.call-start = ((), (), s32[]{:S(2)}) async-start(), calls=%async_computation.6 | async-start | bytes 34078720
  330.4 318.4 %copy-start.1 = (f32[1,512,640]{2,1,0:T(8,128)S(1)}, f32[1,512,640]{2,1,0:T(8,128)}, u32[]{:S(2)}) copy-start(f32[1,512,640]{2,1,0:T(8,128)} %param.21) | copy-start | bytes 3932164
  648.8 7.7 copy-start.11
  648.8 3.7 copy-start.37
  649.0 10.1 copy-start.9
  650.4 13.1 collective-permute-start
  652.5 2.1 collective-permute-start.1
  659.1 4.3 copy-start.17
  666.4 3.3 copy-start
  1232.0 9.5 copy-start.2
  1241.5 3.6 copy-start.13
  1241.5 3.6 copy-start.15
  1241.5 3.6 copy-start.6
  1250.9 5.1 copy-start.7
  1250.9 10.6 slice-start
  1256.0 5.5 slice-start.1
  1261.4 2.5 copy-start.19
  1265.3 14.8 collective-permute-start.2
  1268.9 2.6 copy-start.20
  1268.9 2.6 copy-start.4
  1268.9 2.6 copy-start.18
  1271.5 2.8 copy-start.16
  1282.8 869.8 %reduce-scatter.3.cloned.1.call-start = ((), (), s32[]{:S(2)}) async-start(), calls=%async_computation.3 | async-start | bytes 5283840 | tf_op jit(solution)/shard_map/reduce_scatter | solution.py:197
  1289.0 2.8 copy-start.8
  1291.9 4.7 copy-start.12
  1296.6 70.4 %copy-start.38 = (f32[2,5]{1,0:T(2,128)S(1)}, f32[2,5]{1,0:T(2,128)}, u32[]{:S(2)}) copy-start(f32[2,5]{1,0:T(2,128)} %param.39) | copy-start | bytes 124
  1296.6 70.4 %copy-start.39 = (f32[2,5]{1,0:T(2,128)S(1)}, f32[2,5]{1,0:T(2,128)}, u32[]{:S(2)}) copy-start(f32[2,5]{1,0:T(2,128)} %param.41) | copy-start | bytes 124
  1296.6 70.4 %copy-start.40 = (f32[2,5]{1,0:T(2,128)S(1)}, f32[2,5]{1,0:T(2,128)}, u32[]{:S(2)}) copy-start(f32[2,5]{1,0:T(2,128)} %param.40) | copy-start | bytes 124
  1296.6 71.0 %copy-start.5 = (f32[512,640]{1,0:T(8,128)S(1)}, f32[512,640]{1,0:T(8,128)}, u32[]{:S(2)}) copy-start(f32[512,640]{1,0:T(8,128)} %copy-done.3) | copy-start | bytes 3932164
  1367.6 138.0 %copy-start.28 = (f32[5,512]{1,0:T(8,128)S(1)}, f32[5,512]{1,0:T(8,128)}, u32[]{:S(2)}) copy-start(f32[5,512]{1,0:T(8,128)} %param.27) | copy-start | bytes 30724
  1367.6 138.0 %copy-start.35 = (f32[5,512]{1,0:T(8,128)S(1)}, f32[5,512]{1,0:T(8,128)}, u32[]{:S(2)}) copy-start(f32[5,512]{1,0:T(8,128)} %param.29) | copy-start | bytes 30724
  1367.6 138.0 %copy-start.36 = (f32[5,512]{1,0:T(8,128)S(1)}, f32[5,512]{1,0:T(8,128)}, u32[]{:S(2)}) copy-start(f32[5,512]{1,0:T(8,128)} %param.28) | copy-start | bytes 30724
  1367.6 139.4 %copy-start.27 = (f32[8,640]{1,0:T(8,128)S(1)}, f32[8,640]{1,0:T(8,128)}, u32[]{:S(2)}) copy-start(f32[8,640]{1,0:T(8,128)} %param.30) | copy-start | bytes 61444
  1367.6 139.4 %copy-start.33 = (f32[8,640]{1,0:T(8,128)S(1)}, f32[8,640]{1,0:T(8,128)}, u32[]{:S(2)}) copy-start(f32[8,640]{1,0:T(8,128)} %param.32) | copy-start | bytes 61444
  1367.6 139.4 %copy-start.34 = (f32[8,640]{1,0:T(8,128)S(1)}, f32[8,640]{1,0:T(8,128)}, u32[]{:S(2)}) copy-start(f32[8,640]{1,0:T(8,128)} %param.31) | copy-start | bytes 61444
  1367.7 140.7 %copy-start.26 = (f32[5,1024]{1,0:T(8,128)S(1)}, f32[5,1024]{1,0:T(8,128)}, u32[]{:S(2)}) copy-start(f32[5,1024]{1,0:T(8,128)} %param.24) | copy-start | bytes 61444
  1367.7 140.7 %copy-start.31 = (f32[5,1024]{1,0:T(8,128)S(1)}, f32[5,1024]{1,0:T(8,128)}, u32[]{:S(2)}) copy-start(f32[5,1024]{1,0:T(8,128)} %param.26) | copy-start | bytes 61444
  1367.7 140.7 %copy-start.32 = (f32[5,1024]{1,0:T(8,128)S(1)}, f32[5,1024]{1,0:T(8,128)}, u32[]{:S(2)}) copy-start(f32[5,1024]{1,0:T(8,128)} %param.25) | copy-start | bytes 61444
  1367.7 142.2 %copy-start.21 = (f32[5,4096]{1,0:T(8,128)S(1)}, f32[5,4096]{1,0:T(8,128)}, u32[]{:S(2)}) copy-start(f32[5,4096]{1,0:T(8,128)} %param.33) | copy-start | bytes 245764
  1367.7 142.2 %copy-start.24 = (f32[5,4096]{1,0:T(8,128)S(1)}, f32[5,4096]{1,0:T(8,128)}, u32[]{:S(2)}) copy-start(f32[5,4096]{1,0:T(8,128)} %param.35) | copy-start | bytes 245764
  1367.7 142.2 %copy-start.25 = (f32[5,4096]{1,0:T(8,128)S(1)}, f32[5,4096]{1,0:T(8,128)}, u32[]{:S(2)}) copy-start(f32[5,4096]{1,0:T(8,128)} %param.34) | copy-start | bytes 245764
  1367.7 784.9 %copy-start.23 = (f32[16,640]{1,0:T(8,128)S(1)}, f32[16,640]{1,0:T(8,128)}, u32[]{:S(2)}) copy-start(f32[16,640]{1,0:T(8,128)} %param.36) | copy-start | bytes 122884
  1367.7 784.9 %copy-start.29 = (f32[16,640]{1,0:T(8,128)S(1)}, f32[16,640]{1,0:T(8,128)}, u32[]{:S(2)}) copy-start(f32[16,640]{1,0:T(8,128)} %param.38) | copy-start | bytes 122884
  1367.8 784.9 %copy-start.30 = (f32[16,640]{1,0:T(8,128)S(1)}, f32[16,640]{1,0:T(8,128)}, u32[]{:S(2)}) copy-start(f32[16,640]{1,0:T(8,128)} %param.37) | copy-start | bytes 122884
  (5 other events, 8.4 us)
Sparse Core Ops, SparseCore 0:
  10.3 302.9 all-gather.12
  315.5 294.8 all-gather.8
  612.7 313.1 all-gather.14
  928.0 303.9 all-gather.10
  1283.0 222.6 all-reduce.7
  1507.9 644.6 reduce-scatter.2
where the time goes:
time: 2160 us
  waiting for transfers between devices  1320 us (61%)
  blocking collectives  700 us (32%)
  matrix products  77.8 us (4%)
  other arithmetic  26 us (1%)
    reduce_scatter x1, waiting for transfers between devices, local(): lax.psum_scatter(down_sum, ('seq', 'fsdp'), scatter_dimension=0, tiled=True)  641 us
    all_gather x1, blocking collectives, local(): lax.all_gather(norm_gains.astype(jnp.bfloat16), ('seq', 'fsdp'), axis=1,...  317 us
    all_gather x1, blocking collectives, local(): lax.all_gather(keyval_weight.astype(jnp.bfloat16), ('seq', 'fsdp'), axis=...  316 us
    all_gather x1, waiting for transfers between devices, local(): lax.all_gather(down_weight.astype(jnp.bfloat16), ('seq', 'fsdp'), axis=0,...  289 us
    all_gather x1, waiting for transfers between devices, local(): lax.all_gather(gateup_weight.astype(jnp.bfloat16), ('seq', 'fsdp'), axis=...  250 us
    unnamed x7, waiting for transfers between devices  135 us
    unnamed x1, blocking collectives  68.4 us
    dot_general x16, matrix products, product(): return jnp.einsum(form, left, right, preferred_element_type=jnp.float32)  58.9 us
  transfers between devices with their start and end apart: 9, of which 5 were waited for; matrix products, arithmetic and copies ran while one was open for 4% of the time, Pallas kernels for 0%

commit v1 on v0

v1 whole, which is shorter than its diff:
```python
import functools

import jax
import jax.numpy as jnp
import numpy as np
from jax import lax
from jax.experimental import pallas as pl
from jax.experimental.pallas import tpu as pltpu
from jax.sharding import Mesh, PartitionSpec as P

D = 640
HQ = 4
HD = 256
FF = 2048
WINDOW = 512
STEP = 5
TOK = 512

EPS_NORM = 1e-06
BETA_ONE = 0.9
BETA_TWO = 0.95
ADAM_EPS = 1e-08
DECAY = 0.1
GAIN_RATE = 0.5
RATE_FACTOR = 0.7
MASKED = -1e30

SIZES = {"x": 4, "ylo": 2, "core": 2, "yhi": 2, "z": 4}
OWNERS = ("x", "ylo", "core", "yhi", "z")
SEQ = ("x", "ylo", "core")
FAR = ("x", "yhi", "ylo")
BF = jnp.bfloat16
F32 = jnp.float32

GU_ROWS = 16 * 40
DOWN_ROWS = 5 * 64
OUT_ROWS = 5 * 32
MLP_ROWS = GU_ROWS + DOWN_ROWS
ALL_ROWS = MLP_ROWS + OUT_ROWS
QKV_ROWS = 6 * 40
FIRST_ROWS = QKV_ROWS + 8
QO_ROWS = 160 + OUT_ROWS
KV_ROWS = 80 + 16
Z_GU = 16 * 160
Z_ROWS = Z_GU + 16 * 80
FAR_ROWS = 16 * 10 + 80
VMEM_LIMIT = 22 * 1024 * 1024
MLP_VMEM = 40 * 1024 * 1024
SCALE = HD ** (-0.5)


def dot(left, right):
    return jnp.dot(left, right, preferred_element_type=F32)


def product(form, left, right):
    return jnp.einsum(form, left, right, preferred_element_type=F32)


def adamw_step(weight, mean_old, square_old, gradient, rate, decay):
    mean_new = BETA_ONE * mean_old + (1.0 - BETA_ONE) * gradient
    square_new = BETA_TWO * square_old + (1.0 - BETA_TWO) * gradient * gradient
    mean_hat = mean_new / (1.0 - BETA_ONE**STEP)
    square_hat = square_new / (1.0 - BETA_TWO**STEP)
    weight_new = weight - rate * (mean_hat / (jnp.sqrt(square_hat) + ADAM_EPS) + decay * weight)
    return (mean_new, square_new, weight_new)


def other_core(value):
    return lax.ppermute(value, "core", [(0, 1), (1, 0)])


def by_core(own, other, axis):
    first = lax.axis_index("core") == 0
    return jnp.stack([jnp.where(first, own, other), jnp.where(first, other, own)], axis=axis)


def pick(value, index, axis):
    return lax.dynamic_index_in_dim(value, index, axis, keepdims=False)


def sent_z(value, step):
    return lax.ppermute(value, "z", [(i, (i + step) % 4) for i in range(4)])


def gathered_rows():
    natural = np.arange(D).reshape(4, 2, 2, 2, 4, 5)
    order = natural.transpose(0, 3, 1, 2, 4, 5).reshape(-1)
    out = np.zeros((D, D), np.float32)
    out[order, np.arange(D)] = 1.0
    return out


def gain_rows():
    k = np.arange(D)
    spread = (k[None, :] % 40 == np.arange(128)[:, None]).astype(np.float32)
    keep = (k[None, :] // 40 == np.arange(16)[:, None]).astype(np.float32)
    return spread, keep


def mm(left, right, dims):
    return lax.dot_general(left, right, (dims, ((), ())), preferred_element_type=F32)


NN = ((1,), (0,))
NT = ((1,), (1,))


def natural_columns(value, swap):
    high = value.astype(BF)
    low = (value - high.astype(F32)).astype(BF)
    return mm(high, swap, NT) + mm(low, swap, NT)


def norm_factor(value):
    return lax.rsqrt(jnp.mean(value * value, axis=-1, keepdims=True) + EPS_NORM)


def norm_back(back, value, gain):
    r = norm_factor(value)
    n = value * r
    scaled = back * gain
    return r * (scaled - n * jnp.mean(scaled * n, axis=-1, keepdims=True))


def ordered(first, own, other):
    return jnp.where(first, own, other), jnp.where(first, other, own)


def call(kernel, outs, flops=0, moved=8 << 20, name=None, vmem=VMEM_LIMIT, **kwargs):
    return pl.pallas_call(
        kernel,
        out_shape=[jax.ShapeDtypeStruct(shape, kind) for shape, kind in outs],
        compiler_params=pltpu.CompilerParams(vmem_limit_bytes=vmem),
        cost_estimate=pl.CostEstimate(flops=int(flops), bytes_accessed=moved, transcendentals=0),
        name=name,
        **kwargs,
    )


SMEM = pl.BlockSpec(memory_space=pltpu.SMEM)
VMEM = pl.BlockSpec(memory_space=pltpu.VMEM)


def whole(shape):
    return pl.BlockSpec(shape, lambda *i: (0,) * len(shape))


HALF = 80 + 20 + 10 + 2
PACKED = 2 * HALF + 80 + 40


def scale_kernel(x, ids, scaled):
    value = x[...]
    scaled[:TOK, :] = (value * norm_factor(value)).astype(BF)
    line = jnp.concatenate([ids[...].astype(F32), jnp.zeros((1, D - TOK), F32)], axis=1)
    scaled[TOK:, :] = jnp.broadcast_to(line, (16, D)).astype(BF)


def scale(x, ids):
    return call(scale_kernel, [((TOK + 16, D), BF)], name="scale")(x, ids)[0]


def pack_kernel(core, *refs):
    sources, (out, send, rows, *held, sems) = refs[:6], refs[6:]
    copies = [
        pltpu.make_async_copy(source, ref, sems.at[k])
        for k, (source, ref) in enumerate(zip(sources, held))
    ]
    for copy in copies:
        copy.start()
    gateup, query, keyval, down, output, gains = held
    first = core[0] == 0
    for copy in copies:
        copy.wait()
    gu = gateup[...]
    qs = query[...]
    kvs = keyval[...]
    rows[...] = jnp.zeros_like(rows)
    for t in range(16):
        part, x_at, yhi = t // 8, (t // 2) % 4, t % 2
        pair = []
        for c in range(2):
            at = [part * FF + (((x_at * 2 + ylo) * 2 + c) * 2 + yhi) * 64 for ylo in range(2)]
            pair.append(jnp.concatenate([gu[:, a : a + 64] for a in at], axis=1))
        for base, value in zip((0, HALF), ordered(first, *pair)):
            rows[base + 5 * t : base + 5 * t + 5, :] = value
    for t in range(6):
        if t < 4:
            pair = [qs[:, (c * 4 + t) * 128 : (c * 4 + t + 1) * 128] for c in range(2)]
        else:
            pair = [kvs[:, (c * 2 + t - 4) * 128 : (c * 2 + t - 3) * 128] for c in range(2)]
        for base, value in zip((80, HALF + 80), ordered(first, *pair)):
            rows[base + 5 * t : base + 5 * t + 5, :] = value
    for base, value in zip((110, HALF + 110), ordered(first, gains[0:1, :], gains[1:2, :])):
        rows[base : base + 1, :5] = value
    for t in range(5):
        at = 2 * HALF + t * 16
        rows[at : at + 16, :] = down[:, t * 128 : (t + 1) * 128]
        at = 2 * HALF + 80 + t * 8
        rows[at : at + 8, :] = output[:, t * 128 : (t + 1) * 128]
    out[:HALF, :] = rows[:HALF, :].astype(BF)
    out[HALF:, :] = rows[2 * HALF :, :].astype(BF)
    send[...] = rows[HALF : 2 * HALF, :].astype(BF)


def pack(core, gateup, query, keyval, down, output, gains):
    return call(
        pack_kernel,
        [((PACKED - HALF, 128), BF), ((HALF, 128), BF)],
        name="pack",
        vmem=60 * 1024 * 1024,
        in_specs=[SMEM] + [pl.BlockSpec(memory_space=pltpu.HBM)] * 6,
        scratch_shapes=[pltpu.VMEM((PACKED, 128), F32)]
        + [
            pltpu.VMEM(array.shape, F32)
            for array in (gateup, query, keyval, down, output, gains)
        ]
        + [pltpu.SemaphoreType.DMA((6,))],
    )(core, gateup, query, keyval, down, output, gains)


def layout_kernel(words, near, one, two, three, mlp, head, pieces, rows):
    first = words[0] == 0
    for step, ref in enumerate((near, one, two, three)):
        value = ref[...].astype(F32)
        halves = ordered(first, value[:HALF], value[PACKED - HALF :])
        pieces[lax.rem(words[2] + 4 - step, 4)] = jnp.concatenate(
            [*halves, value[HALF : PACKED - HALF]], axis=0
        )
    line = jnp.zeros((8, 128), F32)
    for z in range(4):
        for c in range(2):
            base = c * HALF
            for t in range(16):
                at = t * 40 + c * 20 + z * 5
                rows[at : at + 5, :] = pieces[z, base + 5 * t : base + 5 * t + 5, :]
            for t in range(6):
                at = ALL_ROWS + t * 40 + c * 20 + z * 5
                rows[at : at + 5, :] = pieces[z, base + 80 + 5 * t : base + 85 + 5 * t, :]
            gain = jnp.broadcast_to(pieces[z, base + 110 : base + 111, :], (8, 128))
            line += pltpu.roll(gain, c * 20 + z * 5, 1)
        for t in range(5):
            at = GU_ROWS + t * 64 + z * 16
            rows[at : at + 16, :] = pieces[z, 2 * HALF + 16 * t : 2 * HALF + 16 * t + 16, :]
            at = MLP_ROWS + t * 32 + z * 8
            rows[at : at + 8, :] = pieces[z, 2 * HALF + 80 + 8 * t : 2 * HALF + 88 + 8 * t, :]
    row = lax.broadcasted_iota(jnp.int32, (8, 128), 0)
    rows[ALL_ROWS + QKV_ROWS :, :] = jnp.where(row == 0, line, 0.0)
    mlp[...] = rows[:ALL_ROWS, :].astype(BF)
    head[...] = rows[ALL_ROWS:, :].astype(BF)


def lay_out(words, near, got):
    return call(
        layout_kernel,
        [((ALL_ROWS, 128), BF), ((FIRST_ROWS, 128), BF)],
        name="lay_out",
        in_specs=[SMEM] + [VMEM] * 4,
        scratch_shapes=[
            pltpu.VMEM((4, PACKED, 128), F32),
            pltpu.VMEM((ALL_ROWS + FIRST_ROWS, 128), F32),
        ],
    )(words, near, *got)


def wide_tiles(rows, tiles):
    return jnp.concatenate(
        [rows[:, t * 40 : (t + 1) * 40, :].reshape(D, 128) for t in range(tiles)], axis=1
    )


def tall_tiles(value, tiles):
    return jnp.concatenate(
        [value[:, t * 128 : (t + 1) * 128].reshape(16, 40, 128) for t in range(tiles)], axis=1
    )


def first_kernel(
    words, x, before, ids, own, other, swap, spread, keep, hidden, q, kv, wq, wkv, gains, gathered, row, column
):
    first = words[0] == 0
    own_ids = jnp.broadcast_to(ids[...].astype(F32), (8, TOK))
    old_ids = jnp.broadcast_to(before[TOK : TOK + 1, :TOK].astype(F32), (8, TOK))
    row[...] = jnp.concatenate([jnp.where(words[1] > 0, old_ids, -1.0), own_ids], axis=1)
    column[...] = own_ids.T

    def gain_row(ref):
        lanes = jnp.sum(ref[:, QKV_ROWS:, :].astype(F32), axis=1).astype(BF)
        return jnp.sum(mm(lanes, spread[...], NN) * keep[...], axis=0, keepdims=True)

    one, two = ordered(first, gain_row(own), gain_row(other))
    both = jnp.concatenate(
        [jnp.broadcast_to(one, (8, D)), jnp.broadcast_to(two, (8, D))], axis=0
    ).astype(BF)
    gathered[...] = both.astype(F32)
    both = mm(both, swap[...], NT)
    gains[...] = both
    value = x[...]
    value = jnp.concatenate([before[:TOK, :].astype(F32), value * norm_factor(value)], axis=0)
    h = (value * both[0:1]).astype(BF)
    h = mm(h, swap[...], NN).astype(BF)
    hidden[...] = h
    mine = wide_tiles(own[...], 6)
    theirs = wide_tiles(other[...], 6)
    w0, w1 = ordered(first, mine, theirs)
    weight = jnp.concatenate([w0[:, :512], w1[:, :512]], axis=1)
    wq[...] = weight
    q[...] = (mm(h[TOK:], weight, NN) * SCALE).astype(BF)
    weight = jnp.concatenate([w0[:, 512:], w1[:, 512:]], axis=1)
    wkv[...] = weight
    kv[...] = mm(h, weight, NN).astype(BF)


def project(words, x, before, ids, own, other, swap, spread, keep):
    outs = [
        ((2 * TOK, D), BF),
        ((TOK, 1024), BF),
        ((2 * TOK, 512), BF),
        ((D, 1024), BF),
        ((D, 512), BF),
        ((16, D), F32),
        ((16, D), F32),
        ((8, 2 * TOK), F32),
        ((TOK, 8), F32),
    ]
    specs = [SMEM] + [pl.BlockSpec(memory_space=pltpu.VMEM)] * 8
    return call(first_kernel, outs, 2 * TOK * D * 3400, name="project", in_specs=specs)(
        words, x, before, ids, own, other, swap, spread, keep
    )


QB = 128
BLOCKS = 2
SPAN = WINDOW + QB
ROW_PART = 64


def stacked(value):
    return jnp.concatenate([value[:, h * HD : (h + 1) * HD] for h in range(HQ)], axis=0)


def side_by_side(value):
    return jnp.concatenate([value[h * QB : (h + 1) * QB] for h in range(HQ)], axis=1)


def window_bias(ids, ids_all, step):
    at = pl.ds(pl.multiple_of(step * QB, QB), SPAN)
    key = lax.broadcasted_iota(jnp.int32, (QB, SPAN), 1)
    token = lax.broadcasted_iota(jnp.int32, (QB, SPAN), 0)
    seen = (key > token) & (key <= token + WINDOW) & (ids == ids_all[0:1, at])
    return jnp.where(seen, 0.0, MASKED)


def window_probs(q, keys, ids, ids_all, step):
    bias = window_bias(ids, ids_all, step)
    scores = mm(q, keys, NT) + jnp.concatenate([bias] * HQ, axis=0)
    exponent = jnp.exp(scores - jnp.max(scores, axis=-1, keepdims=True))
    return exponent / jnp.sum(exponent, axis=-1, keepdims=True)


def attend_kernel(q, both, ids, ids_all, out):
    for k in range(BLOCKS):
        block = pl.program_id(0) * BLOCKS + k
        rows = slice(k * QB, (k + 1) * QB)
        at = pl.ds(pl.multiple_of(block * QB, QB), SPAN)
        probs = window_probs(stacked(q[rows, :]), both[at, :HD], ids[rows, 0:1], ids_all, block)
        out[rows, :] = side_by_side(mm(probs.astype(BF), both[at, HD:], NN)).astype(BF)


def rows_of(width):
    return pl.BlockSpec((BLOCKS * QB, width), lambda i: (i, 0))


def attend(q, both, ids, ids_all):
    return call(
        attend_kernel,
        [((TOK, 1024), BF)],
        4 * TOK * HQ * SPAN * HD,
        name="attend",
        grid=(TOK // QB // BLOCKS,),
        in_specs=[rows_of(1024), VMEM, rows_of(8), VMEM],
        out_specs=[rows_of(1024)],
    )(q, both, ids, ids_all)[0]


def attend_back_kernel(q, back, both, ids, ids_all, dq, old, own, sums, scores, values, low_p, low_s):
    step = pl.program_id(0)

    @pl.when(step == 0)
    def _():
        sums[...] = jnp.zeros_like(sums)

    for k in range(BLOCKS):
        block = step * BLOCKS + k
        rows = slice(k * QB, (k + 1) * QB)
        at = pl.ds(pl.multiple_of(block * QB, QB), SPAN)
        keys = both[at, :HD]
        queries = stacked(q[rows, :])
        attended_back = stacked(back[rows, :])
        scores[k] = mm(queries, keys, NT)
        values[k] = mm(attended_back, both[at, HD:], NT)
        bias = window_bias(ids[rows, 0:1], ids_all, block)
        for first in range(0, HQ * QB, ROW_PART):
            part = slice(first, first + ROW_PART)
            token = first % QB
            raw = scores[k, part, :] + bias[token : token + ROW_PART]
            exponent = jnp.exp(raw - jnp.max(raw, axis=-1, keepdims=True))
            probs = exponent / jnp.sum(exponent, axis=-1, keepdims=True)
            prob_back = values[k, part, :]
            mean = jnp.sum(probs * prob_back, axis=-1, keepdims=True)
            low_p[k, part, :] = probs.astype(BF)
            low_s[k, part, :] = (probs * (prob_back - mean)).astype(BF)
        scores_back = low_s[k]
        dq[rows, :] = side_by_side(mm(scores_back, keys, NN) * SCALE).astype(BF)
        sums[at, :HD] += mm(scores_back.T, queries, NN)
        sums[at, HD:] += mm(low_p[k].T, attended_back, NN)

    @pl.when(step == TOK // QB // BLOCKS - 1)
    def _():
        old[...] = sums[:TOK, :].astype(BF)
        own[...] = sums[TOK:, :].astype(BF)


def attend_back(q, back, both, ids, ids_all):
    return call(
        attend_back_kernel,
        [((TOK, 1024), BF), ((TOK, 512), BF), ((TOK, 512), BF)],
        10 * TOK * HQ * SPAN * HD,
        name="attend_back",
        grid=(TOK // QB // BLOCKS,),
        in_specs=[
            rows_of(1024),
            rows_of(1024),
            VMEM,
            rows_of(8),
            VMEM,
        ],
        out_specs=[rows_of(1024), VMEM, VMEM],
        scratch_shapes=[
            pltpu.VMEM((2 * TOK, 512), F32),
            pltpu.VMEM((BLOCKS, HQ * QB, SPAN), F32),
            pltpu.VMEM((BLOCKS, HQ * QB, SPAN), F32),
            pltpu.VMEM((BLOCKS, HQ * QB, SPAN), BF),
            pltpu.VMEM((BLOCKS, HQ * QB, SPAN), BF),
        ],
    )(q, back, both, ids, ids_all)


def z_first():
    n = lax.broadcasted_iota(jnp.int32, (D, 128), 0)
    shard = (n * 205) >> 10
    z, yhi, core = shard & 3, (shard >> 2) & 1, (shard >> 3) & 1
    ylo, x = (shard >> 4) & 1, shard >> 5
    place = ((((z * 4 + x) * 2 + yhi) * 2 + ylo) * 2 + core) * 5 + n - 5 * shard
    column = lax.broadcasted_iota(jnp.int32, (D, 128), 1)
    tiles = [jnp.where(place == column + t * 128, 1.0, 0.0) for t in range(5)]
    return jnp.concatenate(tiles, axis=1).astype(BF)


def middle_kernel(x, attended, weights, gains, swap, cot, middle, h2, h2t, wo, db):
    w0, w1 = weights[0], weights[1]
    for x_at in range(4):
        for ylo in range(2):
            for c, rows in ((0, w0), (1, w1)):
                for yhi in range(2):
                    place = (x_at * 2 + yhi) * 2 + ylo
                    at = (((x_at * 2 + ylo) * 2 + c) * 2 + yhi) * 32
                    wo[at : at + 32, :] = jnp.concatenate(
                        [rows[place, t * 32 : (t + 1) * 32, :] for t in range(5)], axis=1
                    )
    value = x[...] + mm(attended[...], wo[...], NN)
    middle[...] = value
    h = (value * norm_factor(value) * gains[8:9, :]).astype(BF)
    h2[...] = mm(h, swap[...], NN).astype(BF)
    h2t[...] = mm(h, z_first(), NN).astype(BF).T
    db[...] = cot[...].astype(BF)


def to_middle(x, attended, weights, gains, swap, cot):
    outs = [((TOK, D), F32), ((TOK, D), BF), ((D, TOK), BF), ((1024, D), BF), ((TOK, D), BF)]
    return call(middle_kernel, outs, 2 * TOK * D * 1700, name="to_middle")(
        x, attended, weights, gains, swap, cot
    )


def middle_back_kernel(
    two, middle, h2, gains, gathered, cot, swap, wo, back, branch, attended_back, gain_sum
):
    two_back = natural_columns(two[...], swap[...])
    through = norm_back(two_back, middle[...], gains[8:9, :])
    terms = jnp.sum(two[...] * h2[...].astype(F32), axis=0, keepdims=True) / gathered[8:9, :]
    total = cot[...] + through
    back[...] = total
    branch[...] = total.astype(BF)
    attended_back[...] = mm(total.astype(BF), wo[...], NT).astype(BF)
    gain_sum[...] = jnp.broadcast_to(terms, (8, D))


def to_middle_back(two, middle, h2, gains, gathered, cot, swap, wo):
    outs = [((TOK, D), F32), ((TOK, D), BF), ((TOK, 1024), BF), ((8, D), F32)]
    return call(middle_back_kernel, outs, 2 * TOK * D * 2400, name="middle_back")(
        two, middle, h2, gains, gathered, cot, swap, wo
    )


def query_grad_kernel(core, dq, hidden, wq, attended, branch, own, other, one):
    first = core[0] == 0
    queries_back = dq[...]
    one[...] = mm(queries_back, wq[...], NT)
    sums = mm(hidden[TOK:, :].T, queries_back, NN).astype(BF)
    s_own, s_other = ordered(first, sums[:, :512], sums[:, 512:])
    own[:, :160, :] = tall_tiles(s_own, 4)
    other[:, :160, :] = tall_tiles(s_other, 4)
    sums = mm(attended[...].T, branch[...], NN).astype(BF)
    for x_at in range(4):
        for ylo in range(2):
            for yhi in range(2):
                place = (x_at * 2 + yhi) * 2 + ylo
                at = (((x_at * 2 + ylo) * 2) * 2 + yhi) * 32
                s_own, s_other = ordered(
                    first, sums[at : at + 32, :], sums[at + 64 : at + 96, :]
                )
                for t in range(5):
                    row = 160 + t * 32
                    own[place, row : row + 32, :] = s_own[:, t * 128 : (t + 1) * 128]
                    other[place, row : row + 32, :] = s_other[:, t * 128 : (t + 1) * 128]


def query_grad(core, dq, hidden, wq, attended, branch):
    outs = [((16, QO_ROWS, 128), BF), ((16, QO_ROWS, 128), BF), ((TOK, D), F32)]
    specs = [SMEM] + [pl.BlockSpec(memory_space=pltpu.VMEM)] * 5
    return call(
        query_grad_kernel, outs, 6 * TOK * D * 1024, name="query_grad", in_specs=specs
    )(core, dq, hidden, wq, attended, branch)


def last_kernel(core, old, kept, hidden, wkv, one, gathered, spread, keep, gain_two, own, other, total):
    first = core[0] == 0
    dkv = jnp.concatenate([old[...], kept[...]], axis=0)
    sums = mm(hidden[...].T, dkv, NN).astype(BF)
    s_own, s_other = ordered(first, sums[:, :256], sums[:, 256:])
    own[:, :80, :] = tall_tiles(s_own, 2)
    other[:, :80, :] = tall_tiles(s_other, 2)
    terms = mm(dkv, wkv[...], NT)
    one_own = one[...] + terms[TOK:]
    total[...] = one_own
    gain_sum = jnp.sum(one_own * hidden[TOK:, :].astype(F32), axis=0, keepdims=True)
    gain_sum += jnp.sum(terms[:TOK] * hidden[:TOK, :].astype(F32), axis=0, keepdims=True)
    g_own, g_other = ordered(first, gain_sum / gathered[0:1, :], gain_two[0:1, :])
    row = lax.broadcasted_iota(jnp.int32, (16, 16, 128), 1)
    for ref, line in ((own, g_own), (other, g_other)):
        lanes = mm((keep[...] * line).astype(BF), spread[...], NT)
        ref[:, 80:, :] = jnp.where(row == 0, lanes[:, None, :], 0.0).astype(BF)


def last_grad(core, old, kept, hidden, wkv, one, gathered, spread, keep, gain_two):
    outs = [((16, KV_ROWS, 128), BF), ((16, KV_ROWS, 128), BF), ((TOK, D), F32)]
    return call(
        last_kernel,
        outs,
        2 * TOK * D * 2100,
        name="last_grad",
        in_specs=[SMEM] + [pl.BlockSpec(memory_space=pltpu.VMEM)] * 9,
    )(core, old, kept, hidden, wkv, one, gathered, spread, keep, gain_two)


def input_kernel(one, came_back, wkv, swap, x, gains, middle_back, grad):
    one_back = natural_columns(one[...] + mm(came_back[...], wkv[...], NT), swap[...])
    grad[...] = middle_back[...] + norm_back(one_back, x[...], gains[0:1, :])


def to_input(one, came_back, wkv, swap, x, gains, middle_back):
    return call(input_kernel, [((TOK, D), F32)], 2 * TOK * D * 1800, name="to_input")(
        one, came_back, wkv, swap, x, gains, middle_back
    )[0]


NEAR_ROWS = 32 + 32 + 40


def order_kernel(part, out, rows, moved):
    rows[...] = part[:Z_GU, :].astype(F32)
    for place in range(16):
        for t in range(16):
            at = t * 160 + place * 10
            moved[place, t * 10 : t * 10 + 10, :] = rows[at : at + 10, :]
    out[:, :160, :] = moved[...].astype(BF)
    out[:, 160:, :] = part[Z_GU:, :].reshape(16, 80, 128)


def places_first(part):
    return call(
        order_kernel,
        [((16, FAR_ROWS, 128), BF)],
        name="places_first",
        scratch_shapes=[pltpu.VMEM((Z_GU, 128), F32), pltpu.VMEM((16, 160, 128), F32)],
    )(part)[0]


def parts_kernel(words, firsts, kept, *refs):
    *sends, rows, head = refs
    first = words[0] == 0
    head[...] = jnp.sum(firsts[...].astype(F32), axis=0)
    for z in range(4):
        for c in range(2):
            base = c * 32
            for t in range(6):
                at = (t * 40 if t < 4 else QO_ROWS + (t - 4) * 40) + c * 20 + z * 5
                rows[z, base + 5 * t : base + 5 * t + 5, :] = head[at : at + 5, :]
            lanes = pltpu.roll(head[QO_ROWS + 80 : QO_ROWS + 88, :], (128 - c * 20 - z * 5) % 128, 1)
            rows[z, base + 30 : base + 32, :] = lanes[0:2, :]
        for t in range(5):
            at = 160 + t * 32 + z * 8
            rows[z, 64 + t * 8 : 72 + t * 8, :] = head[at : at + 8, :]
    for step, ref in enumerate((kept, *sends)):
        value = rows[lax.rem(words[2] + step, 4)]
        halves = ordered(first, value[:32], value[32:64])
        ref[...] = jnp.concatenate([*halves, value[64:]], axis=0).astype(ref.dtype)


def near_parts(words, firsts):
    return call(
        parts_kernel,
        [((NEAR_ROWS, 128), F32)] + [((NEAR_ROWS, 128), BF)] * 3,
        name="near_parts",
        in_specs=[SMEM, pl.BlockSpec(memory_space=pltpu.VMEM)],
        scratch_shapes=[
            pltpu.VMEM((4, NEAR_ROWS, 128), F32),
            pltpu.VMEM((QO_ROWS + KV_ROWS, 128), F32),
        ],
    )(words, firsts)


def total_kernel(words, kept, one, two, three, parts, own, send, rows, halves):
    first = words[0] == 0
    near = kept[...] + sum(ref[...].astype(F32) for ref in (one, two, three))
    rows[...] = jnp.sum(parts[...].astype(F32), axis=0)
    for c in range(2):
        for t in range(16):
            at = t * 10 + c * 5
            halves[c, t * 5 : t * 5 + 5, :] = rows[at : at + 5, :]
    mine, theirs = ordered(first, halves[0], halves[1])
    own[...] = jnp.concatenate([mine, near[:32], rows[160:, :], near[64:]], axis=0)
    send[...] = jnp.concatenate([theirs, near[32:64]], axis=0).astype(BF)


def near_total(words, kept, got, parts):
    outs = [((PACKED - HALF, 128), F32), ((HALF, 128), BF)]
    return call(
        total_kernel,
        outs,
        name="near_total",
        in_specs=[SMEM] + [pl.BlockSpec(memory_space=pltpu.VMEM)] * 5,
        scratch_shapes=[pltpu.VMEM((FAR_ROWS, 128), F32), pltpu.VMEM((2, 80, 128), F32)],
    )(words, kept, *got, parts)


def adamw_kernel(words, own, got, *refs):
    olds, news = refs[:18], refs[18:]
    first = words[0] == 0
    halves = ordered(first, own[:HALF, :], got[...].astype(F32))
    pieces = []
    for part in range(2):
        for x_at in range(4):
            for ylo in range(2):
                for c in range(2):
                    pair = [5 * ((part * 4 + x_at) * 2 + yhi) for yhi in range(2)]
                    pieces += [halves[c][a : a + 5, ylo * 64 : ylo * 64 + 64] for a in pair]
    gateup = jnp.concatenate(pieces, axis=1)
    query = [halves[c][80 + 5 * t : 85 + 5 * t] for c in range(2) for t in range(4)]
    keyval = [halves[c][100 + 5 * t : 105 + 5 * t] for c in range(2) for t in range(2)]
    down = [own[HALF + 16 * t : HALF + 16 * t + 16, :] for t in range(5)]
    output = [own[HALF + 80 + 8 * t : HALF + 88 + 8 * t, :] for t in range(5)]
    gains = jnp.concatenate([halves[c][110:111, :5] for c in range(2)], axis=0)
    rate = RATE_FACTOR * D ** (-0.5)
    steps = (
        (jnp.concatenate(query, axis=1), rate, DECAY),
        (jnp.concatenate(keyval, axis=1), rate, DECAY),
        (jnp.concatenate(output, axis=1), RATE_FACTOR * (HQ * HD // WINDOW) ** (-0.5), DECAY),
        (gateup, rate, DECAY),
        (jnp.concatenate(down, axis=1), RATE_FACTOR * FF ** (-0.5), DECAY),
        (gains, GAIN_RATE, 0.0),
    )
    for k, (gradient, rate, decay) in enumerate(steps):
        weight, mean, square = (ref[...] for ref in olds[3 * k : 3 * k + 3])
        new = adamw_step(weight, mean, square, gradient, rate, decay)
        for ref, value in zip(news[3 * k : 3 * k + 3], new):
            ref[...] = value


def adamw_all(words, own, got, arrays):
    outs = [(arrays[3 * k].shape, F32) for k in range(6) for _ in range(3)]
    return call(
        adamw_kernel,
        outs,
        name="adamw",
        vmem=60 * 1024 * 1024,
        in_specs=[SMEM] + [pl.BlockSpec(memory_space=pltpu.VMEM)] * 20,
    )(words, own, got, *arrays)


GELU_K = 0.7978845608028654
GELU_A = 0.044715
STEP_TILES = 2
FF_STEPS = 8 // STEP_TILES


def mlp_kernel(which, h2, h2t, db, gate_w, up_w, down_w, *refs):
    del which
    *sums_in, out, two, grads, gates, ups, inner_backs, inners, gate_backs, up_backs = refs
    step = pl.program_id(0)
    n = STEP_TILES

    @pl.when(step == 0)
    def _():
        out[...] = sums_in[0][...]
        two[...] = sums_in[1][...] if len(sums_in) > 1 else jnp.zeros_like(two)

    wg = wide_tiles(gate_w[...], n)
    wu = wide_tiles(up_w[...], n)
    wd = jnp.concatenate(
        [
            jnp.concatenate([down_w[c, t * 64 : (t + 1) * 64, :] for t in range(5)], axis=1)
            for c in range(2 * n)
        ],
        axis=0,
    )
    hidden = h2[...]
    back = db[...]
    gates[...] = mm(hidden, wg, NN)
    ups[...] = mm(hidden, wu, NN)
    inner_backs[...] = mm(back, wd, NT)
    for first in range(0, TOK, ROW_PART):
        part = slice(first, first + ROW_PART)
        gate, up, inner_back = gates[part, :], ups[part, :], inner_backs[part, :]
        square = gate * gate
        half = 0.5 + 0.5 * jnp.tanh(gate * (GELU_K + GELU_K * GELU_A * square))
        gelu = gate * half
        slope = half + (gelu - gelu * half) * (2.0 * GELU_K + 6.0 * GELU_K * GELU_A * square)
        inners[part, :] = (gelu * up).astype(BF)
        gate_backs[part, :] = (inner_back * up * slope).astype(BF)
        up_backs[part, :] = (inner_back * gelu).astype(BF)
    inner, gate_back, up_back = inners[...], gate_backs[...], up_backs[...]
    out[...] += mm(inner, wd, NN)
    two[...] += mm(gate_back, wg, NT) + mm(up_back, wu, NT)
    dg = mm(h2t[...], gate_back, ((1,), (0,))).astype(BF)
    du = mm(h2t[...], up_back, ((1,), (0,))).astype(BF)
    dd = mm(inner.T, back, NN).astype(BF)
    for t in range(n):
        lanes = slice(t * 128, (t + 1) * 128)
        at = pl.multiple_of((step * n + t) * 160, 160)
        grads[:, pl.ds(at, 160), :] = dg[:, lanes].reshape(4, 160, 128)
        grads[:, pl.ds(Z_GU // 2 + at, 160), :] = du[:, lanes].reshape(4, 160, 128)
        for ylo in range(2):
            at = pl.multiple_of(Z_GU + ((step * n + t) * 2 + ylo) * 80, 80)
            for z in range(4):
                part = dd[t * 128 + ylo * 64 + z * 16 : t * 128 + ylo * 64 + z * 16 + 16, :]
                grads[z, pl.ds(at, 80), :] = jnp.concatenate(
                    [part[:, k * 128 : (k + 1) * 128] for k in range(5)], axis=0
                )


def mlp_half(which, h2, h2t, db, weights, *sums_in):
    n = STEP_TILES
    return pl.pallas_call(
        mlp_kernel,
        grid_spec=pltpu.PrefetchScalarGridSpec(
            num_scalar_prefetch=1,
            grid=(FF_STEPS,),
            in_specs=[
                VMEM,
                VMEM,
                VMEM,
                pl.BlockSpec((None, 16, n * 40, 128), lambda i, w: (w[0], 0, i, 0)),
                pl.BlockSpec((None, 16, n * 40, 128), lambda i, w: (w[0], 0, FF_STEPS + i, 0)),
                pl.BlockSpec((None, 2 * n, DOWN_ROWS, 128), lambda i, w: (w[0], i, 2, 0)),
            ]
            + [VMEM] * len(sums_in),
            out_specs=[VMEM, VMEM, VMEM],
            scratch_shapes=[pltpu.VMEM((TOK, n * 128), F32)] * 3
            + [pltpu.VMEM((TOK, n * 128), BF)] * 3,
        ),
        out_shape=[
            jax.ShapeDtypeStruct((TOK, D), F32),
            jax.ShapeDtypeStruct((TOK, D), F32),
            jax.ShapeDtypeStruct((4, Z_ROWS, 128), BF),
        ],
        compiler_params=pltpu.CompilerParams(vmem_limit_bytes=MLP_VMEM),
        cost_estimate=pl.CostEstimate(
            flops=18 * TOK * D * 1024, bytes_accessed=16 << 20, transcendentals=TOK * 1024
        ),
        name="mlp_half",
    )(which, h2, h2t, db, weights, weights, weights, *sums_in)


def local(
    block_in,
    seg_ids,
    cotangent,
    query_weight,
    query_mean,
    query_square,
    keyval_weight,
    keyval_mean,
    keyval_square,
    output_weight,
    output_mean,
    output_square,
    gateup_weight,
    gateup_mean,
    gateup_square,
    down_weight,
    down_mean,
    down_square,
    norm_gains,
    gains_mean,
    gains_square,
):
    tokens_in = block_in[0]
    core = lax.axis_index("core")
    core_word = core.reshape(1).astype(jnp.int32)
    spread, keep = (jnp.asarray(part) for part in gain_rows())
    spread = spread.astype(BF)

    swap = jnp.asarray(gathered_rows(), BF)
    has_before = (lax.axis_index(SEQ) > 0).astype(jnp.int32)
    words = jnp.stack([core.astype(jnp.int32), has_before, lax.axis_index("z").astype(jnp.int32)])

    mine, send = pack(
        core_word, gateup_weight, query_weight, keyval_weight, down_weight, output_weight, norm_gains
    )
    near = jnp.concatenate([mine, other_core(send)], axis=0)
    got = [sent_z(near, step) for step in (1, 2, 3)]
    mlp_block, first_block = lay_out(words, near, got)

    weights = lax.all_gather(mlp_block, ("core",) + FAR, axis=0, tiled=False)
    weights = weights.reshape(2, 16, ALL_ROWS, 128)
    first_block, scaled = lax.optimization_barrier((first_block, scale(tokens_in, seg_ids)))
    before = lax.ppermute(scaled, SEQ, [(i, i + 1) for i in range(15)])
    first_own = lax.all_gather(first_block, FAR, axis=0, tiled=False)
    first_own, before = lax.optimization_barrier((first_own, before))
    first_other = other_core(first_own)
    upstream = cotangent[0]

    hidden_one, queries, keyvals, wq, wkv, gains_all, gains_gathered, ids_all, ids = project(
        words, tokens_in, before, seg_ids, first_own, first_other, swap, spread, keep
    )
    attended = attend(queries, keyvals, ids, ids_all)

    weights, attended = lax.optimization_barrier((weights, attended))
    middle, hidden_two, hidden_two_t, wo, down_back = to_middle(
        tokens_in, attended, weights[:, :, MLP_ROWS:], gains_all, swap, upstream
    )
    out_part, two_part, grads_other = mlp_half(
        1 - core_word, hidden_two, hidden_two_t, down_back, weights, middle
    )
    grads_there = other_core(grads_other)
    block_out, two_back, grads_own = mlp_half(
        core_word, hidden_two, hidden_two_t, down_back, weights, out_part, two_part
    )
    grads_both = (grads_own.astype(F32) + grads_there.astype(F32)).astype(BF)
    mlp_part = lax.psum_scatter(
        grads_both.reshape(4 * Z_ROWS, 128), "z", scatter_dimension=0, tiled=True
    )

    middle_back, branch_back, attended_back, gain_two_sum = to_middle_back(
        two_back, middle, hidden_two, gains_all, gains_gathered, upstream, swap, wo
    )
    queries_back, old_back, kept_back = attend_back(queries, attended_back, keyvals, ids, ids_all)
    came_back = lax.ppermute(old_back, SEQ, [(i + 1, i) for i in range(15)])
    qo_own, qo_other, one_part = query_grad(
        core_word, queries_back, hidden_one, wq, attended, branch_back
    )
    qo_there = other_core(qo_other)
    kv_own, kv_other, one_part = last_grad(
        core_word,
        old_back,
        kept_back,
        hidden_one,
        wkv,
        one_part,
        gains_gathered,
        spread,
        keep,
        gain_two_sum,
    )
    kv_there = other_core(kv_other)
    sums_both = jnp.concatenate(
        [
            (mine.astype(F32) + there.astype(F32)).astype(BF)
            for mine, there in ((qo_own, qo_there), (kv_own, kv_there))
        ],
        axis=1,
    )
    first_part = lax.all_to_all(sums_both, FAR, 0, 0, tiled=True)
    moved, came_back = lax.optimization_barrier((places_first(mlp_part), came_back))
    mlp_far = lax.all_to_all(moved, FAR, 0, 0, tiled=True)

    kept, *sends = near_parts(words, first_part)
    kept, came_back = lax.optimization_barrier((kept, came_back))
    input_grad = to_input(one_part, came_back, wkv, swap, tokens_in, gains_all, middle_back)
    kept, input_grad = lax.optimization_barrier((kept, input_grad))
    own_sum, other_sum = near_total(
        words, kept, [sent_z(sends[k], k + 1) for k in range(3)], mlp_far
    )
    news = adamw_all(
        words,
        own_sum,
        other_core(other_sum),
        (
            query_weight,
            query_mean,
            query_square,
            keyval_weight,
            keyval_mean,
            keyval_square,
            output_weight,
            output_mean,
            output_square,
            gateup_weight,
            gateup_mean,
            gateup_square,
            down_weight,
            down_mean,
            down_square,
            norm_gains,
            gains_mean,
            gains_square,
        ),
    )
    return (block_out[None], input_grad[None], *news)


def solution(mesh):
    fine = Mesh(mesh.devices.reshape([SIZES[a] for a in OWNERS]), OWNERS)
    tokens = P(("yhi", "z"), SEQ, None)
    rows = P(OWNERS, None)
    columns = P(None, OWNERS)
    return jax.shard_map(
        local,
        mesh=fine,
        in_specs=(tokens, P(("yhi", "z"), SEQ), tokens) + (rows,) * 15 + (columns,) * 3,
        out_specs=(tokens, tokens) + (rows,) * 15 + (columns,) * 3,
        check_vma=False,
    )
```

time: 2160 us -> 205 us (0.09)
  waiting for transfers between devices: 1320 us -> 40.4 us
  blocking collectives: 700 us -> 26.9 us
  matrix products: 77.8 us -> 0 us
  Pallas kernels: 0 us -> 58 us
  starting transfers between devices: 5.12 us -> 32.6 us
    reduce_scatter x1, waiting for transfers between devices: 641 us -> 13.3 us  [local(): lax.psum_scatter(grads_both.reshape(4 * Z_ROWS, 128), 'z', scatter_dimens...]
    all_gather x2 -> x1, blocking collectives: 632 us -> 26.9 us  [local(): first_own = lax.all_gather(first_block, FAR, axis=0, tiled=False)]
    all_gather x4 -> x1, waiting for transfers between devices: 539 us -> 2.95 us  [local(): weights = lax.all_gather(mlp_block, ('core',) + FAR, axis=0, tiled=False)]
    unnamed x7 -> x2, waiting for transfers between devices: 135 us -> 0.03 us
    dot_general x21 -> x0, matrix products: 77.8 us -> none  [the longest x16 58.9 us: product(): return jnp.einsum(form, left, right, preferred_element_type=jnp.float32)]
    unnamed x1 -> x0, blocking collectives: 68.4 us -> none
    pallas_call x0 -> x17, Pallas kernels: none -> 58 us  [the longest x2 20.7 us: mlp_half(): pl.pallas_call(mlp_kernel, grid_spec=pltpu.PrefetchScalarGridSpec(num_sca...]
  transfers between devices with their start and end apart: 9 -> 18, of which waited for: 5 -> 11; matrix products, arithmetic and copies ran while one was open for 4% -> 1% of each run, Pallas kernels for 0% -> 19%
where the time goes in v1:
time: 205 us; the launch traced here: 203 us
  Pallas kernels  58 us (28%)
  waiting for transfers between devices  40.4 us (20%)
  starting transfers between devices  32.6 us (16%)
  blocking collectives  26.9 us (13%)
  local copies, waits for them, and re-layouts  25.7 us (13%)
  between operations  14.5 us (7%)
  other arithmetic  4.85 us (2%)
    all_gather x1, blocking collectives, local(): first_own = lax.all_gather(first_block, FAR, axis=0, tiled=False)  26.9 us
    unnamed x91, local copies, waits for them, and re-layouts  24.2 us
    pallas_call x2, Pallas kernels, mlp_half(): pl.pallas_call(mlp_kernel, grid_spec=pltpu.PrefetchScalarGridSpec(num_sca...  20.7 us
    reduce_scatter x1, waiting for transfers between devices, local(): lax.psum_scatter(grads_both.reshape(4 * Z_ROWS, 128), 'z', scatter_dimens...  13.3 us
    ppermute x6, starting transfers between devices, sent_z(): return lax.ppermute(value, 'z', [(i, (i + step) % 4) for i in range(4)])  10.8 us
    all_to_all x1, waiting for transfers between devices, local(): first_part = lax.all_to_all(sums_both, FAR, 0, 0, tiled=True)  8.91 us
    pallas_call x1, Pallas kernels, attend_back(): call(attend_back_kernel, [((TOK, 1024), BF), ((TOK, 512), BF), ((TOK, 512...  7.14 us
    ppermute x6, starting transfers between devices, other_core(): return lax.ppermute(value, 'core', [(0, 1), (1, 0)])  6.86 us
  transfers between devices with their start and end apart: 18, of which 11 were waited for; matrix products, arithmetic and copies ran while one was open for 1% of the time, Pallas kernels for 19%

profile of v1, /device:TPU:0, one launch (start us, length us, event | category | flops | bytes accessed | tf_op | source)
XLA Modules:
  0.0 203.0 jit_solution(17180157040217538780)
XLA Ops:
  7.2 1.7 pack.1
  10.5 4.1 %collective-permute-start.3 = (bf16[344,128]{1,0:T(8,128)(2,1)S(1)}, bf16[344,128]{1,0:T(8,128)(2,1)S(1)}, u32[]{:S(2)}, u32[]{:S(2)}) collective-permute-start(bf16[344,128]{1,0:T(8,128)(2,1)S(1)} %constant_dynamic-update-slice_fusion.near), channel_id=1, source_target_pairs={{0,3},{1,0},{2,1},{3,2},{4,7},{5,4},{6,5},{7,6},{8,11},{9,8},{10,9... | collective-permute-start | bytes 264200 | tf_op jit(solution)/shard_map/ppermute | solution.py:83
  14.6 1.3 collective-permute-start.1
  15.9 2.7 %collective-permute-done.3.three = bf16[344,128]{1,0:T(8,128)(2,1)S(1)} collective-permute-done((bf16[344,128]{1,0:T(8,128)(2,1)S(1)}, bf16[344,128]{1,0:T(8,128)(2,1)S(1)}, u32[]{:S(2)}, u32[]{:S(2)}) %collective-permute-start.3) | collective-permute-done | bytes 88096 | tf_op jit(solution)/shard_map/ppermute | solution.py:83
  18.6 2.8 %collective-permute-done.2.two = bf16[344,128]{1,0:T(8,128)(2,1)S(1)} collective-permute-done((bf16[344,128]{1,0:T(8,128)(2,1)S(1)}, bf16[344,128]{1,0:T(8,128)(2,1)S(1)}, u32[]{:S(2)}, u32[]{:S(2)}) %collective-permute-start.2) | collective-permute-done | bytes 88096 | tf_op jit(solution)/shard_map/ppermute | solution.py:83
  22.1 1.4 lay_out.1
  23.6 1.3 copy-done
  25.7 1.8 collective-permute-start.4
  27.5 26.9 %all-gather.1 = bf16[3968,128]{1,0:T(8,128)(2,1)S(1)} all-gather(bf16[248,128]{1,0:T(8,128)(2,1)S(1)} %get-tuple-element.97), channel_id=3, replica_groups=mesh['x'=4,'ylo'=2,'core'=2,'yhi'=2,'z'=4] {'x','yhi','ylo'}, dimensions={0}, use_global_device_ids=true | all-gather | bytes 1079296 | tf_op jit(solution)/shard_map/all_gather | solution.py:841
  54.5 5.0 %collective-permute-start.5 = (bf16[16,248,128]{2,1,0:T(8,128)(2,1)S(1)}, bf16[16,248,128]{2,1,0:T(8,128)(2,1)S(1)}, u32[]{:S(2)}, u32[]{:S(2)}) collective-permute-start(bf16[16,248,128]{2,1,0:T(8,128)(2,1)S(1)} %bitcast.16), channel_id=1, source_target_pairs={{0,8},{8,0},{1,9},{9,1},{2,10},{10,2},{3,11},{11,3},{4,12},{12,4},... | collective-permute-start | bytes 3047432 | tf_op jit(solution)/shard_map/ppermute | solution.py:70
  59.5 2.2 %collective-permute-done.5.other = bf16[16,248,128]{2,1,0:T(8,128)(2,1)S(1)} collective-permute-done((bf16[16,248,128]{2,1,0:T(8,128)(2,1)S(1)}, bf16[16,248,128]{2,1,0:T(8,128)(2,1)S(1)}, u32[]{:S(2)}, u32[]{:S(2)}) %collective-permute-start.5) | collective-permute-done | bytes 1015840 | tf_op jit(solution)/shard_map/ppermute | solution.py:70
  61.8 3.9 %project.1 = (bf16[1024,640]{1,0:T(8,128)(2,1)S(1)}, bf16[512,1024]{1,0:T(8,128)(2,1)S(1)}, bf16[1024,512]{1,0:T(8,128)(2,1)S(1)}, bf16[640,1024]{1,0:T(8,128)(2...) custom-call(s32[3]{0:T(128)S(1)} %pad_add_fusion.words, ...), custom_call_target="tpu_custom_call" | custom-call | flops 2228224000 | bytes 8388608 | tf_op jit(solution)/shard_map/project/pallas_call | solution.py:328
  65.7 1.1 copy-done.32
  66.8 1.1 copy-done.38
  67.9 3.6 %attend.1.attended = bf16[512,1024]{1,0:T(8,128)(2,1)S(1)} custom-call(bf16[512,1024]{1,0:T(8,128)(2,1)S(1)} %get-tuple-element.101.q, bf16[1024,512]{1,0:T(8,128)(2,1)S(1)} %get-tuple-element.102.both, f32[512,8]{1,0:T(8,128)S(1)} %get-tuple-element.103.ids, f32[8,1024]{1,0:T(8,128)S(1)} %get-tuple-element.104.ids_all), custom_call_target="tpu_custom_call" | custom-call | flops 1342177280 | bytes 8388608 | tf_op jit(solution)/shard_map/attend/pallas_call | solution.py:376
  75.8 2.9 %all-gather.4.cloned.1.call-done = bf16[35840,128]{1,0:T(8,128)(2,1)} async-done(((bf16[1120,128]{1,0:T(8,128)(2,1)}), bf16[35840,128]{1,0:T(8,128)(2,1)}) %all-gather.4.cloned.1.call-update) | async-done | bytes 9175056 | tf_op jit(solution)/shard_map/all_gather | solution.py:837
  78.8 1.6 slice.3.weights
  80.9 1.2 copy-done.16
  82.1 2.4 %to_middle.1 = (f32[512,640]{1,0:T(8,128)S(1)}, bf16[512,640]{1,0:T(8,128)(2,1)S(1)}, bf16[640,512]{1,0:T(8,128)(2,1)S(1)}, bf16[1024,640]{1,0:T(8,128)(2,1)S(1)}, bf16[512,640]{1,0:T(8,128)(2,1)S(1)}) custom-call(f32[512,640]{1,0:T(8,128)S(1)} %bitcast.12, bf16[512,1024]{1,0:T(8,128)(2,1)S(1)} %copy-done.16, bf16[2,16,160,128]{3,2,1,0:T(8,128)(2,1)S(1)} %slice.3.weights, ...), custom_call_target="tpu_custom_call" | custom-call | flops 1114112000 | bytes 8388608 | tf_op jit(solution)/shard_map/to_middle/pallas_call | solution.py:482
  85.6 10.2 %mlp_half.2 = (f32[512,640]{1,0:T(8,128)S(1)}, f32[512,640]{1,0:T(8,128)S(1)}, bf16[4,3840,128]{2,1,0:T(8,128)(2,1)S(1)}) custom-call(s32[1]{0:T(128)S(6)} %sub.3.which, bf16[512,640]{1,0:T(8,128)(2,1)S(1)} %get-tuple-element.108.h2, bf16[640,512]{1,0:T(8,128)(2,1)S(1)} %get-tuple-element.109.h2t, bf16[512,640]{1,0:T(8,128)(2,1)S(1)} %get-tuple-element.110.db, ...), custom_call_target="tpu_custom_call" | custom-call | flops 6039797760 | bytes 16777216 | tf_op jit(solution)/shard_map/mlp_half/pallas_call | solution.py:766
  96.3 10.5 %mlp_half.3 = (f32[512,640]{1,0:T(8,128)}, f32[512,640]{1,0:T(8,128)S(1)}, bf16[4,3840,128]{2,1,0:T(8,128)(2,1)S(1)}) custom-call(s32[1]{0:T(128)} %bitcast.core.which, bf16[512,640]{1,0:T(8,128)(2,1)S(1)} %get-tuple-element.108.h2, bf16[640,512]{1,0:T(8,128)(2,1)S(1)} %get-tuple-element.109.h2t, bf16[512,640]{1,0:T(8,128)(2,1)S(1)} %get-tuple-element.110.db, ...), custom_call_target="tpu_custom_call" | custom-call | flops 6039797760 | bytes 16777216 | tf_op jit(solution)/shard_map/mlp_half/pallas_call | solution.py:766
  106.8 3.0 %add_convert_fusion = bf16[4,3840,128]{2,1,0:T(8,128)(2,1)} fusion(bf16[4,3840,128]{2,1,0:T(8,128)(2,1)S(1)} %collective-permute-done.8, bf16[4,3840,128]{2,1,0:T(8,128)(2,1)S(1)} %get-tuple-element.133), kind=kLoop, calls=%fused_computation | loop fusion | flops 7864320 | bytes 11796480 | tf_op jit(solution)/shard_map/convert_element_type | solution.py:862
  109.8 1.3 copy-done.4
  111.1 1.3 copy-done.6
  112.4 1.3 copy-done.8
  113.7 1.3 copy-done.10
  115.1 2.8 %middle_back.1 = (f32[512,640]{1,0:T(8,128)S(1)}, bf16[512,640]{1,0:T(8,128)(2,1)S(1)}, bf16[512,1024]{1,0:T(8,128)(2,1)S(1)}, f32[8,640]{1,0:T(8,128)S(1)}) custom-call(f32[512,640]{1,0:T(8,128)S(1)} %copy-done.10, f32[512,640]{1,0:T(8,128)S(1)} %copy-done.4, bf16[512,640]{1,0:T(8,128)(2,1)S(1)} %get-tuple-element.108.h2, ...), custom_call_target="tpu_custom_call" | custom-call | flops 1572864000 | bytes 8388608 | tf_op jit(solution)/shard_map/middle_back/pallas_call | solution.py:502
  118.0 7.1 %attend_back.1 = (bf16[512,1024]{1,0:T(8,128)(2,1)S(1)}, bf16[512,512]{1,0:T(8,128)(2,1)S(1)}, bf16[512,512]{1,0:T(8,128)(2,1)S(1)}) custom-call(bf16[512,1024]{1,0:T(8,128)(2,1)S(1)} %copy-done.35, bf16[512,1024]{1,0:T(8,128)(2,1)S(1)} %get-tuple-element.118.back, bf16[1024,512]{1,0:T(8,128)(2,1)S(1)} %copy-done.37, f32[512,8]{1,0:T(8,128)S(1)} %copy-done.41, ...), custom_call_target="tpu_custom_call" | custom-call | flops 3355443200 | bytes 8388608 | tf_op jit(solution)/shard_map/attend_back/pallas_call | solution.py:426
  125.2 2.6 %query_grad.1 = (bf16[16,320,128]{2,1,0:T(8,128)(2,1)S(1)}, bf16[16,320,128]{2,1,0:T(8,128)(2,1)S(1)}, f32[512,640]{1,0:T(8,128)S(1)}) custom-call(s32[1]{0:T(128)} %bitcast.core.which, bf16[512,1024]{1,0:T(8,128)(2,1)S(1)} %get-tuple-element.119.dq, bf16[1024,640]{1,0:T(8,128)(2,1)S(1)} %copy-done.33, bf16[640,1024]{1,0:T(8,128)(2,1)S(1)} %copy-done.39, ...), custom_call_target="tpu_custom_call" | custom-call | flops 2013265920 | bytes 8388608 | tf_op jit(solution)/shard_map/query_grad/pallas_call | solution.py:533
  128.4 2.0 %last_grad.1 = (bf16[16,96,128]{2,1,0:T(8,128)(2,1)S(1)}, bf16[16,96,128]{2,1,0:T(8,128)(2,1)S(1)}, f32[512,640]{1,0:T(8,128)S(1)}) custom-call(s32[1]{0:T(128)} %bitcast.core.which, bf16[512,512]{1,0:T(8,128)(2,1)S(1)} %get-tuple-element.125.old, bf16[512,512]{1,0:T(8,128)(2,1)S(1)} %get-tuple-element.126.kept, bf16[1024,640]{1,0:T(8,128)(2,1)S(1)} %copy-done.33, ...), custom_call_target="tpu_custom_call" | custom-call | flops 1376256000 | bytes 8388608 | tf_op jit(solution)/shard_map/last_grad/pallas_call | solution.py:559
  130.8 1.5 collective-permute-done.7
  132.7 1.3 pad_maximum_fusion
  134.1 5.1 %all-to-all-start = ((bf16[16,416,128]{2,1,0:T(8,128)(2,1)}), bf16[16,416,128]{2,1,0:T(8,128)(2,1)}, u32[]{:S(2)}, u32[]{:S(2)}) async-start(bf16[16,416,128]{2,1,0:T(8,128)(2,1)} %pad_maximum_fusion), calls=%async_computation | async-start | bytes 3407872 | tf_op jit(solution)/shard_map/all_to_all | solution.py:896
  139.2 1.3 collective-permute-start.9
  140.5 13.3 %reduce-scatter.2.cloned.1.call-done.part = bf16[3840,128]{1,0:T(8,128)(2,1)} async-done(((bf16[15360,128]{1,0:T(8,128)(2,1)}), bf16[3840,128]{1,0:T(8,128)(2,1)}) %reduce-scatter.2.cloned.1.call-update) | async-done | bytes 983056 | tf_op jit(solution)/shard_map/reduce_scatter | solution.py:863
  153.8 1.2 copy-done.18
  155.0 1.3 places_first.1
  157.0 8.9 %all-to-all-done.firsts = bf16[16,416,128]{2,1,0:T(8,128)(2,1)} async-done(((bf16[16,416,128]{2,1,0:T(8,128)(2,1)}), bf16[16,416,128]{2,1,0:T(8,128)(2,1)}, u32[]{:S(2)}, u32[]{:S(2)}) %all-to-all-start) | async-done | bytes 1703968 | tf_op jit(solution)/shard_map/all_to_all | solution.py:896
  165.9 6.7 %all-to-all-start.1 = ((bf16[16,240,128]{2,1,0:T(8,128)(2,1)}), bf16[16,240,128]{2,1,0:T(8,128)(2,1)S(1)}, u32[]{:S(2)}, u32[]{:S(2)}) async-start(bf16[16,240,128]{2,1,0:T(8,128)(2,1)} %places_first.1), calls=%async_computation.2 | async-start | bytes 1966080 | tf_op jit(solution)/shard_map/all_to_all | solution.py:898
  172.7 1.9 near_parts.1
  174.6 1.2 collective-permute-start.10
  175.7 2.9 %collective-permute-start.11 = (bf16[104,128]{1,0:T(8,128)(2,1)S(1)}, bf16[104,128]{1,0:T(8,128)(2,1)S(1)}, u32[]{:S(2)}, u32[]{:S(2)}) collective-permute-start(bf16[104,128]{1,0:T(8,128)(2,1)S(1)} %get-tuple-element.143), channel_id=1, source_target_pairs={{0,2},{1,3},{2,0},{3,1},{4,6},{5,7},{6,4},{7,5},{8,10},{9,11},{10,... | collective-permute-start | bytes 79880 | tf_op jit(solution)/shard_map/ppermute | solution.py:83
  178.6 1.4 collective-permute-start.12
  180.0 1.3 copy-done.14
  181.3 1.1 copy-done.20
  183.4 3.3 %to_input.1 = f32[512,640]{1,0:T(8,128)} custom-call(f32[512,640]{1,0:T(8,128)S(1)} %copy-done.14, bf16[512,512]{1,0:T(8,128)(2,1)S(1)} %copy-done.22, bf16[640,512]{1,0:T(8,128)(2,1)S(1)} %copy-done.20, bf16[640,640]{1,0:T(8,128)(2,1)S(1)} %copy-done.2, f32[512,640]{1,0:T(8,128)S(1)} %bitcast.13, f32[16,640]{1,0:T(8,128)S(1)} %get-tuple-element.107.gains, ...), custom_call_target="tpu_custom_call" | custom-call | flops 1179648000 | bytes 8388608 | tf_op jit(solution)/shard_map/to_input/pallas_call | solution.py:574
  186.7 4.0 %all-to-all-done.1.parts = bf16[16,240,128]{2,1,0:T(8,128)(2,1)S(1)} async-done(((bf16[16,240,128]{2,1,0:T(8,128)(2,1)}), bf16[16,240,128]{2,1,0:T(8,128)(2,1)S(1)}, u32[]{:S(2)}, u32[]{:S(2)}) %all-to-all-start.1) | async-done | bytes 983072 | tf_op jit(solution)/shard_map/all_to_all | solution.py:898
  193.9 2.3 %adamw.1 = (f32[5,1024]{1,0:T(8,128)}, f32[5,1024]{1,0:T(8,128)}, f32[5,1024]{1,0:T(8,128)}, f32[5,512]{1,0:T(8,128)}, f32[5,512]{1,0:T(8,128)}, /*index=5*/f32[...) custom-call(s32[3]{0:T(128)} %copy-done.24, ...), custom_call_target="tpu_custom_call" | custom-call | bytes 8388608 | tf_op jit(solution)/shard_map/adamw/pallas_call | solution.py:694
  (106 shorter events, 16.1 us)
Async XLA Ops:
  7.2 71.6 %all-gather.4.cloned.1.call-start = ((), (), s32[]{:S(2)}) async-start(), calls=%async_computation.4 | async-start | bytes 9461760 | tf_op jit(solution)/shard_map/all_gather | solution.py:837
  9.0 1.5 collective-permute-start
  10.5 8.2 %collective-permute-start.3 = (bf16[344,128]{1,0:T(8,128)(2,1)S(1)}, bf16[344,128]{1,0:T(8,128)(2,1)S(1)}, u32[]{:S(2)}, u32[]{:S(2)}) collective-permute-start(bf16[344,128]{1,0:T(8,128)(2,1)S(1)} %constant_dynamic-update-slice_fusion.near), channel_id=1, source_target_pairs={{0,3},{1,0},{2,1},{3,2},{4,7},{5,4},{6,5},{7,6},{8,11},{9,8},{10,9... | collective-permute-start | bytes 264200 | tf_op jit(solution)/shard_map/ppermute | solution.py:83
  14.6 6.8 %collective-permute-start.2 = (bf16[344,128]{1,0:T(8,128)(2,1)S(1)}, bf16[344,128]{1,0:T(8,128)(2,1)S(1)}, u32[]{:S(2)}, u32[]{:S(2)}) collective-permute-start(bf16[344,128]{1,0:T(8,128)(2,1)S(1)} %constant_dynamic-update-slice_fusion.near), channel_id=1, source_target_pairs={{0,2},{1,3},{2,0},{3,1},{4,6},{5,7},{6,4},{7,5},{8,10},{9,11},{10,... | collective-permute-start | bytes 264200 | tf_op jit(solution)/shard_map/ppermute | solution.py:83
  14.6 7.5 %collective-permute-start.1 = (bf16[344,128]{1,0:T(8,128)(2,1)S(1)}, bf16[344,128]{1,0:T(8,128)(2,1)S(1)}, u32[]{:S(2)}, u32[]{:S(2)}) collective-permute-start(bf16[344,128]{1,0:T(8,128)(2,1)S(1)} %constant_dynamic-update-slice_fusion.near), channel_id=1, source_target_pairs={{0,1},{1,2},{2,3},{3,0},{4,5},{5,6},{6,7},{7,4},{8,9},{9,10},{10,1... | collective-permute-start | bytes 264200 | tf_op jit(solution)/shard_map/ppermute | solution.py:83
  15.9 174.8 %copy-start.24 = (s32[3]{0:T(128)}, s32[3]{0:T(128)S(1)}, u32[]{:S(2)}) copy-start(s32[3]{0:T(128)S(1)} %pad_add_fusion.words) | copy-start | bytes 40
  23.5 130.3 %reduce-scatter.2.cloned.1.call-start = ((), (), s32[]{:S(2)}) async-start(), calls=%async_computation.3 | async-start | bytes 4915200 | tf_op jit(solution)/shard_map/reduce_scatter | solution.py:863
  23.5 1.3 copy-start
  25.5 36.2 %copy-start.2 = (bf16[640,640]{1,0:T(8,128)(2,1)S(1)}, bf16[640,640]{1,0:T(8,128)(2,1)}, u32[]{:S(2)}) copy-start(bf16[640,640]{1,0:T(8,128)(2,1)} %constant.33.clone.swap) | copy-start | bytes 2457604
  25.5 36.2 %copy-start.28 = (bf16[128,640]{1,0:T(8,128)(2,1)S(1)}, bf16[128,640]{1,0:T(8,128)(2,1)}, u32[]{:S(2)}) copy-start(bf16[128,640]{1,0:T(8,128)(2,1)} %constant.55.spread) | copy-start | bytes 491524
  25.6 36.2 %copy-start.30 = (f32[16,640]{1,0:T(8,128)S(1)}, f32[16,640]{1,0:T(8,128)}, u32[]{:S(2)}) copy-start(f32[16,640]{1,0:T(8,128)} %constant.32.clone.keep) | copy-start | bytes 122884
  25.7 28.7 %collective-permute-start.4 = (bf16[528,640]{1,0:T(8,128)(2,1)S(1)}, bf16[528,640]{1,0:T(8,128)(2,1)S(1)}, u32[]{:S(2)}, u32[]{:S(2)}) collective-permute-start(bf16[528,640]{1,0:T(8,128)(2,1)S(1)} %scale.1), channel_id=1, source_target_pairs={{0,8},{8,16},{16,24},{24,32},{32,40},{40,48},{48,56},{56,64},{64,7... | collective-permute-start | bytes 2027528 | tf_op jit(solution)/shard_map/ppermute | solution.py:840
  54.5 7.3 %collective-permute-start.5 = (bf16[16,248,128]{2,1,0:T(8,128)(2,1)S(1)}, bf16[16,248,128]{2,1,0:T(8,128)(2,1)S(1)}, u32[]{:S(2)}, u32[]{:S(2)}) collective-permute-start(bf16[16,248,128]{2,1,0:T(8,128)(2,1)S(1)} %bitcast.16), channel_id=1, source_target_pairs={{0,8},{8,0},{1,9},{9,1},{2,10},{10,2},{3,11},{11,3},{4,12},{12,4},... | collective-permute-start | bytes 3047432 | tf_op jit(solution)/shard_map/ppermute | solution.py:70
  67.9 60.5 %copy-start.19 = (bf16[640,512]{1,0:T(8,128)(2,1)}, bf16[640,512]{1,0:T(8,128)(2,1)S(1)}, u32[]{:S(2)}) copy-start(bf16[640,512]{1,0:T(8,128)(2,1)S(1)} %get-tuple-element.127.wkv) | copy-start | bytes 1966084
  78.8 1.7 copy-start.1
  78.8 2.1 %copy-start.5 = (f32[1,512,640]{2,1,0:T(8,128)S(1)}, f32[1,512,640]{2,1,0:T(8,128)}, u32[]{:S(2)}) copy-start(f32[1,512,640]{2,1,0:T(8,128)} %param.26) | copy-start | bytes 3932164
  80.9 1.2 copy-start.16
  85.6 10.2 %copy-start.3 = (f32[512,640]{1,0:T(8,128)}, f32[512,640]{1,0:T(8,128)S(1)}, u32[]{:S(2)}) copy-start(f32[512,640]{1,0:T(8,128)S(1)} %get-tuple-element.111.refs_0_.middle) | copy-start | bytes 3932164
  95.7 11.0 %collective-permute-start.8 = (bf16[4,3840,128]{2,1,0:T(8,128)(2,1)S(1)}, bf16[4,3840,128]{2,1,0:T(8,128)(2,1)S(1)}, u32[]{:S(2)}, u32[]{:S(2)}) collective-permute-start(bf16[4,3840,128]{2,1,0:T(8,128)(2,1)S(1)} %get-tuple-element.134), channel_id=1, source_target_pairs={{0,8},{8,0},{1,9},{9,1},{2,10},{10,2},{3,11},{11,3},{4,12},{12,4},... | collective-permute-start | bytes 11796488 | tf_op jit(solution)/shard_map/ppermute | solution.py:70
  106.8 3.0 %copy-start.9 = (f32[512,640]{1,0:T(8,128)}, f32[512,640]{1,0:T(8,128)S(1)}, u32[]{:S(2)}) copy-start(f32[512,640]{1,0:T(8,128)S(1)} %get-tuple-element.115.two) | copy-start | bytes 3932164
  109.8 1.3 copy-start.4
  111.1 1.3 copy-start.6
  112.4 1.3 copy-start.8
  113.7 1.3 copy-start.10
  115.0 2.9 %copy-start.35 = (bf16[512,1024]{1,0:T(8,128)(2,1)S(1)}, bf16[512,1024]{1,0:T(8,128)(2,1)}, u32[]{:S(2)}) copy-start(bf16[512,1024]{1,0:T(8,128)(2,1)} %copy-done.34) | copy-start | bytes 3145732
  115.0 2.9 %copy-start.37 = (bf16[1024,512]{1,0:T(8,128)(2,1)S(1)}, bf16[1024,512]{1,0:T(8,128)(2,1)}, u32[]{:S(2)}) copy-start(bf16[1024,512]{1,0:T(8,128)(2,1)} %copy-done.36) | copy-start | bytes 3145732
  115.0 2.9 %copy-start.41 = (f32[512,8]{1,0:T(8,128)S(1)}, f32[512,8]{1,0:T(8,128)}, u32[]{:S(2)}) copy-start(f32[512,8]{1,0:T(8,128)} %copy-done.40) | copy-start | bytes 49156
  115.0 2.9 %copy-start.43 = (f32[8,1024]{1,0:T(8,128)S(1)}, f32[8,1024]{1,0:T(8,128)}, u32[]{:S(2)}) copy-start(f32[8,1024]{1,0:T(8,128)} %copy-done.42) | copy-start | bytes 98308
  117.9 7.2 %copy-start.11 = (f32[512,640]{1,0:T(8,128)}, f32[512,640]{1,0:T(8,128)S(1)}, u32[]{:S(2)}) copy-start(f32[512,640]{1,0:T(8,128)S(1)} %get-tuple-element.139.middle_back) | copy-start | bytes 3932164
  117.9 7.2 %copy-start.17 = (bf16[512,1024]{1,0:T(8,128)(2,1)S(1)}, bf16[512,1024]{1,0:T(8,128)(2,1)}, u32[]{:S(2)}) copy-start(bf16[512,1024]{1,0:T(8,128)(2,1)} %copy-done.15) | copy-start | bytes 3145732
  118.0 7.2 %copy-start.33 = (bf16[1024,640]{1,0:T(8,128)(2,1)S(1)}, bf16[1024,640]{1,0:T(8,128)(2,1)}, u32[]{:S(2)}) copy-start(bf16[1024,640]{1,0:T(8,128)(2,1)} %copy-done.32) | copy-start | bytes 3932164
  118.0 7.2 %copy-start.39 = (bf16[640,1024]{1,0:T(8,128)(2,1)S(1)}, bf16[640,1024]{1,0:T(8,128)(2,1)}, u32[]{:S(2)}) copy-start(bf16[640,1024]{1,0:T(8,128)(2,1)} %copy-done.38) | copy-start | bytes 3932164
  125.1 3.2 %copy-start.26 = (bf16[512,512]{1,0:T(8,128)(2,1)}, bf16[512,512]{1,0:T(8,128)(2,1)S(1)}, u32[]{:S(2)}) copy-start(bf16[512,512]{1,0:T(8,128)(2,1)S(1)} %get-tuple-element.125.old) | copy-start | bytes 1572868
  125.2 3.2 %copy-start.29 = (bf16[128,640]{1,0:T(8,128)(2,1)S(1)}, bf16[128,640]{1,0:T(8,128)(2,1)}, u32[]{:S(2)}) copy-start(bf16[128,640]{1,0:T(8,128)(2,1)} %constant.55.spread) | copy-start | bytes 491524
  125.2 3.2 %copy-start.31 = (f32[16,640]{1,0:T(8,128)S(1)}, f32[16,640]{1,0:T(8,128)}, u32[]{:S(2)}) copy-start(f32[16,640]{1,0:T(8,128)} %constant.32.clone.keep) | copy-start | bytes 122884
  127.8 4.6 %collective-permute-start.6 = (bf16[16,320,128]{2,1,0:T(8,128)(2,1)S(1)}, bf16[16,320,128]{2,1,0:T(8,128)(2,1)S(1)}, u32[]{:S(2)}, u32[]{:S(2)}) collective-permute-start(bf16[16,320,128]{2,1,0:T(8,128)(2,1)S(1)} %get-tuple-element.124), channel_id=1, source_target_pairs={{0,8},{8,0},{1,9},{9,1},{2,10},{10,2},{3,11},{11,3},{4,12},{12,4},... | collective-permute-start | bytes 3932168 | tf_op jit(solution)/shard_map/ppermute | solution.py:70
  130.4 2.3 %copy-start.13 = (f32[512,640]{1,0:T(8,128)}, f32[512,640]{1,0:T(8,128)S(1)}, u32[]{:S(2)}) copy-start(f32[512,640]{1,0:T(8,128)S(1)} %get-tuple-element.137.one) | copy-start | bytes 3932164
  130.4 1.8 collective-permute-start.7
  134.1 5.1 %copy-start.27 = (bf16[512,512]{1,0:T(8,128)(2,1)S(1)}, bf16[512,512]{1,0:T(8,128)(2,1)}, u32[]{:S(2)}) copy-start(bf16[512,512]{1,0:T(8,128)(2,1)} %copy-done.26) | copy-start | bytes 1572868
  134.1 31.9 %all-to-all-start = ((bf16[16,416,128]{2,1,0:T(8,128)(2,1)}), bf16[16,416,128]{2,1,0:T(8,128)(2,1)}, u32[]{:S(2)}, u32[]{:S(2)}) async-start(bf16[16,416,128]{2,1,0:T(8,128)(2,1)} %pad_maximum_fusion), calls=%async_computation | async-start | bytes 3407872 | tf_op jit(solution)/shard_map/all_to_all | solution.py:896
  139.2 17.0 %collective-permute-start.9 = (bf16[512,512]{1,0:T(8,128)(2,1)S(1)}, bf16[512,512]{1,0:T(8,128)(2,1)S(1)}, u32[]{:S(2)}, u32[]{:S(2)}) collective-permute-start(bf16[512,512]{1,0:T(8,128)(2,1)S(1)} %copy-done.27), channel_id=1, source_target_pairs={{8,0},{16,8},{24,16},{32,24},{40,32},{48,40},{56,48},{64,56},{72,6... | collective-permute-start | bytes 1572872 | tf_op jit(solution)/shard_map/ppermute | solution.py:871
  165.9 24.7 %all-to-all-start.1 = ((bf16[16,240,128]{2,1,0:T(8,128)(2,1)}), bf16[16,240,128]{2,1,0:T(8,128)(2,1)S(1)}, u32[]{:S(2)}, u32[]{:S(2)}) async-start(bf16[16,240,128]{2,1,0:T(8,128)(2,1)} %places_first.1), calls=%async_computation.2 | async-start | bytes 1966080 | tf_op jit(solution)/shard_map/all_to_all | solution.py:898
  172.7 7.3 %copy-start.12 = (f32[512,640]{1,0:T(8,128)S(1)}, f32[512,640]{1,0:T(8,128)}, u32[]{:S(2)}) copy-start(f32[512,640]{1,0:T(8,128)} %copy-done.11) | copy-start | bytes 3932164
  174.6 12.1 %collective-permute-start.10 = (bf16[104,128]{1,0:T(8,128)(2,1)S(1)}, bf16[104,128]{1,0:T(8,128)(2,1)S(1)}, u32[]{:S(2)}, u32[]{:S(2)}) collective-permute-start(bf16[104,128]{1,0:T(8,128)(2,1)S(1)} %get-tuple-element.142), channel_id=1, source_target_pairs={{0,1},{1,2},{2,3},{3,0},{4,5},{5,6},{6,7},{7,4},{8,9},{9,10},{10,1... | collective-permute-start | bytes 79880 | tf_op jit(solution)/shard_map/ppermute | solution.py:83
  175.7 11.0 %collective-permute-start.11 = (bf16[104,128]{1,0:T(8,128)(2,1)S(1)}, bf16[104,128]{1,0:T(8,128)(2,1)S(1)}, u32[]{:S(2)}, u32[]{:S(2)}) collective-permute-start(bf16[104,128]{1,0:T(8,128)(2,1)S(1)} %get-tuple-element.143), channel_id=1, source_target_pairs={{0,2},{1,3},{2,0},{3,1},{4,6},{5,7},{6,4},{7,5},{8,10},{9,11},{10,... | collective-permute-start | bytes 79880 | tf_op jit(solution)/shard_map/ppermute | solution.py:83
  178.6 8.1 %collective-permute-start.12 = (bf16[104,128]{1,0:T(8,128)(2,1)S(1)}, bf16[104,128]{1,0:T(8,128)(2,1)S(1)}, u32[]{:S(2)}, u32[]{:S(2)}) collective-permute-start(bf16[104,128]{1,0:T(8,128)(2,1)S(1)} %get-tuple-element.144), channel_id=1, source_target_pairs={{0,3},{1,0},{2,1},{3,2},{4,7},{5,4},{6,5},{7,6},{8,11},{9,8},{10,9... | collective-permute-start | bytes 79880 | tf_op jit(solution)/shard_map/ppermute | solution.py:83
  180.0 1.3 copy-start.14
  192.1 1.2 collective-permute-start.13
  (15 other events, 13.6 us)
Sparse Core Ops, SparseCore 0:
  23.6 55.0 all-gather.3
  109.9 43.8 reduce-scatter.1
